TPU v7x, 128 devices: a whole 4x4x4 slice. The times are simulated.
128 devices in a mesh: tp: 8 (over z, y_lo), req: 16 (over y_hi, x, core).
Axes of the slice: x: 4, y: 4 (y_hi: 2, y_lo: 2; y = y_hi * 2 + y_lo), z: 4, core: 2. Of those that a mesh axis runs over, the one named last changes fastest.
Arguments:
- tokens: bfloat16 [8192, 8192], P('req'), may hold values from -6 to 6
- w_query: bfloat16 [8192, 8, 1024], P('req', 'tp'), may hold values from -1 to 1
- w_keyval: bfloat16 [8192, 8, 256], P(None, 'tp'), may hold values from -1 to 1
- output_weight: bfloat16 [8192, 8, 1024], P('req', 'tp'), may hold values from -0.0625 to 0.0625
- cache: bfloat16 [2, 256, 1024, 1024], P(None, 'req', None, 'tp'), may hold values from -6 to 6
- fresh: bfloat16 [2, 4, 256, 1024], P(None, None, 'req', 'tp'), may hold values from -6 to 6
- decode_query: bfloat16 [4, 256, 8192], P(None, 'req', 'tp'), may hold values from -6 to 6
- cache_len: int32 [16, 16], P('req'), may hold values from 1 to 1024, 10240 in all within a row
- new_len: int32 [16, 16], replicated, may hold values from 1 to 64, 512 in all within a row
- route: int32 [16, 16], replicated, may hold values from 0 to 15, each once within a row
Outputs:
- prefill_out: bfloat16 [8192, 8192], P('req', 'tp')
- decode_out: bfloat16 [4, 256, 8192], P(None, 'req', 'tp')
Inputs may be any that keep to these rules, and one draw needn't show every extreme that they name: `new_len`: each row sums to 512. `cache_len`: each row of one decode group sums to 10240. `route`: each row is a permutation of 0..15.
All inputs are finite; a program needn't handle non-finite values.
Results may differ from a plain program's by a relative error of at most 0.0065.
Values may be sent and summed in bfloat16 or wider, within the bound.
A program may use at most 128 MiB of HBM per device.

v0:
```python
import jax
import jax.numpy as jnp
from jax import lax
from jax.sharding import PartitionSpec as P

NEG = -1e30


def segment_ids(lens, count):
    ends = jnp.cumsum(lens)
    position = jnp.arange(count, dtype=jnp.int32)
    return jnp.sum((position[:, None] >= ends[None, :]).astype(jnp.int32), axis=1)


def prefill_attend(query, keyval, lens):
    count, heads = (keyval.shape[0], keyval.shape[1])
    width = keyval.shape[2] // 2
    group = query.shape[2] // width
    scale = width ** (-0.5)
    seg = segment_ids(lens, count)
    position = jnp.arange(count, dtype=jnp.int32)
    allowed = (seg[:, None] == seg[None, :]) & (position[None, :] <= position[:, None])
    q_four = query.reshape(count, heads, group, width)
    keys = keyval[:, :, :width]
    values = keyval[:, :, width:]
    scores = jnp.einsum("ihgd,jhd->hgij", q_four, keys, preferred_element_type=jnp.float32) * scale
    scores = jnp.where(allowed[None, None], scores, NEG)
    top = jnp.max(scores, axis=-1, keepdims=True)
    expo = jnp.exp(scores - top)
    total = jnp.sum(expo, axis=-1)
    weights = expo.astype(jnp.bfloat16)
    acc = jnp.einsum("hgij,jhd->ihgd", weights, values, preferred_element_type=jnp.float32)
    mixed = acc / jnp.transpose(total, (2, 0, 1))[..., None]
    return mixed.astype(jnp.bfloat16).reshape(count, heads * group * width)


def decode_attend(query, cache, fresh, stretch, cache_rows, stretch_rows):
    steps, rows = (query.shape[0], query.shape[1])
    heads = stretch.shape[2]
    width = stretch.shape[3] // 2
    group = query.shape[2] // (heads * width)
    span = cache.shape[2]
    most = stretch.shape[1]
    scale = width ** (-0.5)
    f32 = jnp.float32
    q_five = query.reshape(steps, rows, heads, group, width)
    ckeys = cache[0].reshape(rows, span, heads, width)
    cvals = cache[1].reshape(rows, span, heads, width)
    nkeys = stretch[..., :width]
    nvals = stretch[..., width:]
    fkeys = fresh[0].reshape(steps, rows, heads, width)
    fvals = fresh[1].reshape(steps, rows, heads, width)
    s_cache = jnp.einsum("trhgd,rchd->rhtgc", q_five, ckeys, preferred_element_type=f32) * scale
    s_new = jnp.einsum("trhgd,rnhd->rhtgn", q_five, nkeys, preferred_element_type=f32) * scale
    s_fresh = jnp.einsum("trhgd,urhd->rhtgu", q_five, fkeys, preferred_element_type=f32) * scale
    mask_cache = jnp.arange(span, dtype=jnp.int32)[None, :] < cache_rows[:, None]
    mask_new = jnp.arange(most, dtype=jnp.int32)[None, :] < stretch_rows[:, None]
    mask_fresh = jnp.arange(steps)[None, :] <= jnp.arange(steps)[:, None]
    s_cache = jnp.where(mask_cache[:, None, None, None, :], s_cache, NEG)
    s_new = jnp.where(mask_new[:, None, None, None, :], s_new, NEG)
    s_fresh = jnp.where(mask_fresh[None, None, :, None, :], s_fresh, NEG)
    top = jnp.maximum(
        jnp.maximum(jnp.max(s_cache, axis=-1), jnp.max(s_new, axis=-1)), jnp.max(s_fresh, axis=-1)
    )[..., None]
    e_cache = jnp.exp(s_cache - top)
    e_new = jnp.exp(s_new - top)
    e_fresh = jnp.exp(s_fresh - top)
    total = jnp.sum(e_cache, axis=-1) + jnp.sum(e_new, axis=-1) + jnp.sum(e_fresh, axis=-1)
    acc = jnp.einsum(
        "rhtgc,rchd->trhgd", e_cache.astype(jnp.bfloat16), cvals, preferred_element_type=f32
    )
    acc = acc + jnp.einsum(
        "rhtgn,rnhd->trhgd", e_new.astype(jnp.bfloat16), nvals, preferred_element_type=f32
    )
    acc = acc + jnp.einsum(
        "rhtgu,urhd->trhgd", e_fresh.astype(jnp.bfloat16), fvals, preferred_element_type=f32
    )
    mixed = acc / jnp.transpose(total, (2, 0, 1, 3))[..., None]
    return mixed.astype(jnp.bfloat16).reshape(steps, rows, heads * group * width)


def local(
    tokens, w_query, w_keyval, output_weight, cache, fresh, decode_query, cache_len, new_len, route
):
    f32 = jnp.float32
    count, model = tokens.shape
    heads = w_keyval.shape[1]
    width = w_keyval.shape[2] // 2
    groups, slots = (route.shape[0], route.shape[1])
    my_group = lax.axis_index("req")
    qcols = w_query.shape[1] * w_query.shape[2]
    piece = lax.all_gather(w_query, "req", axis=0, tiled=True)
    query = jnp.dot(
        tokens, piece.reshape(piece.shape[0], qcols), preferred_element_type=f32
    ).astype(jnp.bfloat16)
    keyval = jnp.dot(tokens, w_keyval.reshape(model, -1), preferred_element_type=f32).astype(
        jnp.bfloat16
    )
    my_lens = lax.dynamic_index_in_dim(new_len, my_group, 0, keepdims=False)
    mixed = prefill_attend(
        query.reshape(count, heads, -1), keyval.reshape(count, heads, 2 * width), my_lens
    )
    piece = lax.all_gather(output_weight, "req", axis=0, tiled=True)
    partial_terms = lax.dot_general(
        mixed,
        piece.reshape(piece.shape[0], qcols),
        (((1,), (1,)), ((), ())),
        preferred_element_type=f32,
    )
    prefill_out = lax.psum_scatter(partial_terms, "tp", scatter_dimension=1, tiled=True).astype(
        jnp.bfloat16
    )
    offsets = jnp.cumsum(my_lens) - my_lens
    my_route = lax.dynamic_index_in_dim(route, my_group, 0, keepdims=False)
    ranks = jnp.arange(groups, dtype=jnp.int32)
    hit_send = (my_route[None, :] == ranks[:, None]).astype(jnp.int32)
    start = jnp.sum(hit_send * offsets[None, :], axis=1)
    most = 2 * count // slots
    cols = keyval.shape[1]
    padded = jnp.concatenate([keyval, jnp.zeros((most, cols), jnp.bfloat16)], axis=0)
    index = start[:, None] + jnp.arange(most, dtype=jnp.int32)[None, :]
    outgoing = padded[index]
    incoming = lax.all_to_all(outgoing, "req", split_axis=0, concat_axis=0, tiled=True)
    hit_recv = (route == my_group).astype(jnp.int32)
    stretch_rows = jnp.sum(hit_recv * new_len, axis=1)
    stretch = incoming.reshape(groups, most, heads, 2 * width)
    decode_out = decode_attend(
        decode_query, cache, fresh, stretch, cache_len.reshape(-1), stretch_rows
    )
    return (prefill_out, decode_out)


def solution(mesh):
    placed = (
        P("req", None),
        P("req", "tp", None),
        P(None, "tp", None),
        P("req", "tp", None),
        P(None, "req", None, "tp"),
        P(None, None, "req", "tp"),
        P(None, "req", "tp"),
        P("req", None),
        P(),
        P(),
    )
    return jax.shard_map(
        local,
        mesh=mesh,
        in_specs=placed,
        out_specs=(P("req", "tp"), P(None, "req", "tp")),
        check_vma=False,
    )
```

profile of v0, /device:TPU:24, one launch (start us, length us, event | category | flops | bytes accessed | tf_op | source)
XLA Modules:
  0.0 588.7 jit_solution(2088757423289404257)
XLA Ops:
  7.2 0.7 all-gather.3.cloned.1.call-update
  7.9 0.7 all-gather.5.cloned.1.call-update
  8.7 0.7 fusion.65
  9.9 6.9 %fusion.31 = bf16[512,256]{1,0:T(8,128)(2,1)S(1)} fusion(bf16[512,8192]{1,0:T(8,128)(2,1)} %param.10, bf16[8192,1,256]{2,0,1:T(8,128)(2,1)} %param.12), kind=kOutput, calls=%fused_computation.30 | convolution fusion | flops 2147614720 | bytes 12845056 | tf_op jit(solution)/shard_map/dot_general | solution.py:96
  16.8 104.4 %all-gather.3.cloned.1.call-done = bf16[8192,1,1024]{2,0,1:T(8,128)(2,1)} async-done(((bf16[512,1,1024]{2,0,1:T(8,128)(2,1)}), bf16[8192,1,1024]{2,0,1:T(8,128)(2,1)}) %all-gather.3.cloned.1.call-update) | async-done | bytes 16777232 | tf_op jit(solution)/shard_map/all_gather | solution.py:92
  121.2 14.8 %fusion.28 = bf16[64,8,8,128]{3,2,1,0:T(8,128)(2,1)S(1)} fusion(bf16[512,8192]{1,0:T(8,128)(2,1)} %param.10, bf16[8192,1,1024]{2,0,1:T(8,128)(2,1)} %all-gather.3.cloned.1.call-done), kind=kOutput, calls=%fused_computation.29 | convolution fusion | flops 8590458880 | bytes 26214400 | tf_op jit(solution)/shard_map/dot_general | solution.py:93
  136.0 1.6 fusion.6
  137.6 1.7 fusion.4
  139.3 2.5 fusion.19
  141.8 89.8 %all-gather.5.cloned.1.call-done = bf16[8192,1,1024]{2,0,1:T(8,128)(2,1)} async-done(((bf16[512,1,1024]{2,0,1:T(8,128)(2,1)}), bf16[8192,1,1024]{2,0,1:T(8,128)(2,1)}) %all-gather.5.cloned.1.call-update) | async-done | bytes 16777232 | tf_op jit(solution)/shard_map/all_gather | solution.py:103
  231.7 15.8 %fusion = f32[512,8192]{1,0:T(8,128)} fusion(bf16[512,1024]{0,1:T(8,128)(2,1)S(1)} %bitcast.197, bf16[8192,1,1024]{2,0,1:T(8,128)(2,1)} %all-gather.5.cloned.1.call-done), kind=kOutput, calls=%fused_computation.1 | convolution fusion | flops 8589934592 | bytes 34603008 | tf_op jit(solution)/shard_map/dot_general | solution.py:104
  247.6 0.6 copy-done.2
  248.5 5.0 gather_fusion
  253.5 5.6 all-to-all-start
  259.4 0.7 fusion.71
  260.2 3.7 fusion.20
  263.9 4.7 all-to-all-done
  268.6 0.3 fusion.72
  269.1 0.3 fusion.53
  269.4 0.6 fusion.23
  270.3 3.2 fusion.34
  273.8 0.7 copy.41
  274.5 305.0 %reduce-scatter.2.cloned.1.call-done = f32[512,1024]{1,0:T(8,128)} async-done(((f32[512,8192]{1,0:T(8,128)}), f32[512,1024]{1,0:T(8,128)}) %reduce-scatter.2.cloned.1.call-update) | async-done | bytes 2097168 | tf_op jit(solution)/shard_map/reduce_scatter | solution.py:110
  579.5 2.7 convert_element_type.40
  (36 shorter events, 2.0 us)
Async XLA Ops:
  7.2 114.0 %all-gather.3.cloned.1.call-start = ((), (), s32[]{:S(2)}) async-start(), calls=%async_computation.2 | async-start | bytes 17825792 | tf_op jit(solution)/shard_map/all_gather | solution.py:92
  7.9 223.8 %all-gather.5.cloned.1.call-start = ((), (), s32[]{:S(2)}) async-start(), calls=%async_computation.3 | async-start | bytes 17825792 | tf_op jit(solution)/shard_map/all_gather | solution.py:103
  8.6 570.8 %reduce-scatter.2.cloned.1.call-start = ((), (), s32[]{:S(2)}) async-start(), calls=%async_computation.4 | async-start | bytes 18874368 | tf_op jit(solution)/shard_map/reduce_scatter | solution.py:110
  247.5 0.7 copy-start.2
  247.5 0.7 copy-start.3
  247.5 11.6 %copy-start = (bf16[4,16,1024]{2,1,0:T(8,128)(2,1)S(1)}, bf16[4,16,1024]{2,1,0:T(8,128)(2,1)}, u32[]{:S(2)}) copy-start(bf16[4,16,1024]{2,1,0:T(8,128)(2,1)} %param.16) | copy-start | bytes 393220
  247.5 11.8 %copy-start.4 = (s32[1,16]{1,0:T(1,128)S(1)}, s32[1,16]{1,0:T(1,128)}, u32[]{:S(2)}) copy-start(s32[1,16]{1,0:T(1,128)} %param.17) | copy-start | bytes 196
  247.5 11.9 %copy-start.1 = (bf16[2,4,16,128]{3,2,1,0:T(8,128)(2,1)S(1)}, bf16[2,4,16,128]{3,2,1,0:T(8,128)(2,1)}, u32[]{:S(2)}) copy-start(bf16[2,4,16,128]{3,2,1,0:T(8,128)(2,1)} %param.15) | copy-start | bytes 98308
  253.5 15.1 %all-to-all-start = ((bf16[16,64,256]{2,1,0:T(8,128)(2,1)}), bf16[16,64,256]{2,1,0:T(8,128)(2,1)S(1)}, u32[]{:S(2)}, u32[]{:S(2)}) async-start(bf16[16,64,256]{2,1,0:T(8,128)(2,1)} %bitcast.24), calls=%async_computation.1 | async-start | bytes 1048576 | tf_op jit(solution)/shard_map/all_to_all | solution.py:123
Sparse Core Ops, SparseCore 0:
  10.4 110.7 all-gather.2
  123.6 107.9 all-gather.4
  247.7 331.7 reduce-scatter.1
where the time goes:
time: 590 us; the launch traced here: 589 us
  waiting for transfers between devices  505 us (86%)
  matrix products  50.1 us (8%)
  between operations  13.9 us (2%)
  local copies, waits for them, and re-layouts  7.3 us (1%)
  other arithmetic  6.49 us (1%)
    reduce_scatter x1, waiting for transfers between devices, local(): lax.psum_scatter(partial_terms, 'tp', scatter_dimension=1, tiled=True)  305 us
    all_gather x1, waiting for transfers between devices, local(): piece = lax.all_gather(w_query, 'req', axis=0, tiled=True)  104 us
    all_gather x1, waiting for transfers between devices, local(): piece = lax.all_gather(output_weight, 'req', axis=0, tiled=True)  89.8 us
    dot_general x1, matrix products, local(): lax.dot_general(mixed, piece.reshape(piece.shape[0], qcols), (((1,), (1,)...  15.8 us
    dot_general x1, matrix products, local(): jnp.dot(tokens, piece.reshape(piece.shape[0], qcols), preferred_element_t...  14.8 us
  transfers between devices with their start and end apart: 4, of which 4 were waited for; matrix products, arithmetic and copies ran while one was open for 8% of the time, Pallas kernels for 0%

commit v1 on v0

--- a/solution.py
+++ b/solution.py
@@ -1,9 +1,476 @@
+import functools
+
 import jax
 import jax.numpy as jnp
 from jax import lax
+from jax.experimental import pallas as pl
+from jax.experimental.pallas import tpu as pltpu
 from jax.sharding import PartitionSpec as P
 
 NEG = -1e30
+MESH = pl.DeviceIdType.MESH
+F32 = jnp.float32
+BF16 = jnp.bfloat16
+
+CUT_Q = 256
+CUT_O = 384
+LAG1 = 1
+LAG2 = 2
+
+MOVES = {
+    "yA": ((0, 0), "A", (0, 1), "y"),
+    "xpA": ((0, 0), "A", (3, 0), "xp"),
+    "xmA": ((0, 0), "A", (1, 0), "xm"),
+    "xpB": ((0, 0), "B", (3, 0), "xp"),
+    "xmB": ((0, 0), "B", (1, 0), "xm"),
+    "xpC": ((0, 1), "A", (3, 1), "xp"),
+    "xmC": ((0, 1), "A", (1, 1), "xm"),
+    "fpA": ((3, 0), "A0", (2, 0), "xp"),
+    "fmA": ((1, 0), "A1", (2, 0), "xm"),
+    "fpB": ((3, 0), "B0", (2, 0), "xp"),
+    "fmB": ((1, 0), "B1", (2, 0), "xm"),
+    "fpC": ((3, 1), "A0", (2, 1), "xp"),
+    "fmC": ((1, 1), "A1", (2, 1), "xm"),
+    "yB0": ((0, 0), "B", (0, 1), "y"),
+    "yBm": ((3, 0), "B", (3, 1), "y"),
+    "yBp": ((1, 0), "B", (1, 1), "y"),
+    "yB2p": ((2, 0), "B0", (2, 1), "y"),
+    "yB2m": ((2, 0), "B1", (2, 1), "y"),
+}
+SLOTS = [(dx, dy) for dy in range(2) for dx in range(4)]
+for _slot in SLOTS:
+    for _part in "AB":
+        MOVES["s%d%d%s" % (_slot + (_part,))] = (_slot, _part, _slot, "sib")
+INDEX = {name: i for i, name in enumerate(MOVES)}
+N_MOVES = len(MOVES)
+FIRST = ["yA", "xpA", "xmA", "s00A", "xpB", "xmB", "yB0", "s00B"]
+EVENTS = [
+    (["yA"], ["xpC", "xmC", "s01A"], [((0, 1), "A")]),
+    (["xpA", "xmA"], ["fpA", "fmA", "s30A", "s10A"], [((3, 0), "A"), ((1, 0), "A")]),
+    (["xpB", "xmB"], ["fpB", "fmB", "yBm", "yBp", "s30B", "s10B"], [((3, 0), "B"), ((1, 0), "B")]),
+    (["xpC", "xmC"], ["fpC", "fmC", "s31A", "s11A"], [((3, 1), "A"), ((1, 1), "A")]),
+    (["fpA", "fmA"], ["s20A"], [((2, 0), "A")]),
+    (["fpB", "fmB"], ["yB2p", "yB2m", "s20B"], [((2, 0), "B")]),
+    (["yB0"], ["s01B"], [((0, 1), "B")]),
+    (["yBm", "yBp"], ["s31B", "s11B"], [((3, 1), "B"), ((1, 1), "B")]),
+    (["fpC", "fmC"], ["s21A"], [((2, 1), "A")]),
+    (["yB2p", "yB2m"], ["s21B"], [((2, 1), "B")]),
+]
+UNITS = [((0, 0), "A"), ((0, 0), "B")] + [u for e in EVENTS for u in e[2]]
+
+
+def where_am_i():
+    tp = lax.axis_index("tp")
+    req = lax.axis_index("req")
+    return tp // 2, tp % 2, req // 8, (req // 2) % 4, req % 2
+
+
+def neighbours():
+    z, ylo, yhi, x, c = where_am_i()
+    tp = z * 2 + ylo
+    req = yhi * 8 + x * 2 + c
+    return {
+        "xp": (tp, yhi * 8 + ((x + 1) % 4) * 2 + c),
+        "xm": (tp, yhi * 8 + ((x + 3) % 4) * 2 + c),
+        "y": (tp, (1 - yhi) * 8 + x * 2 + c),
+        "sib": (tp, yhi * 8 + x * 2 + (1 - c)),
+        "zp": (((z + 1) % 4) * 2 + ylo, req),
+        "zm": (((z + 3) % 4) * 2 + ylo, req),
+        "yl": (z * 2 + (1 - ylo), req),
+    }
+
+
+def row_range(part, cut, rows):
+    rest = rows - cut
+    return {
+        "A": (0, cut),
+        "A0": (0, cut // 2),
+        "A1": (cut // 2, cut // 2),
+        "B": (cut, rest),
+        "B0": (cut, rest // 2),
+        "B1": (cut + rest // 2, rest // 2),
+    }[part]
+
+
+class Gather:
+    def __init__(self, buf, cut, send, recv, near):
+        self.buf, self.cut, self.send, self.recv, self.near = buf, cut, send, recv, near
+
+    def copy(self, name):
+        src, part, dst, way = MOVES[name]
+        start, size = row_range(part, self.cut, self.buf.shape[2])
+        lane = 1 if way == "sib" else 0
+        i = INDEX[name]
+        return pltpu.make_async_remote_copy(
+            src_ref=self.buf.at[0, src[1] * 4 + src[0], pl.ds(start, size)],
+            dst_ref=self.buf.at[lane, dst[1] * 4 + dst[0], pl.ds(start, size)],
+            send_sem=self.send.at[i],
+            recv_sem=self.recv.at[i],
+            device_id=self.near[way],
+            device_id_type=MESH,
+        )
+
+    def start(self, names):
+        for name in names:
+            self.copy(name).start()
+
+    def event(self, k):
+        waits, starts, _ = EVENTS[k]
+        for name in waits:
+            self.copy(name).wait_recv()
+        self.start(starts)
+
+    def shared(self, unit):
+        (dx, dy), part = unit
+        self.copy("s%d%d%s" % (dx, dy, part)).wait_recv()
+
+    def finish(self):
+        for name in MOVES:
+            self.copy(name).wait_send()
+
+
+def layer_kernel(
+    tok_hbm, wq_hbm, wkv_hbm, wo_hbm, bias_ref,
+    out_ref, kv_ref,
+    tok, wq, wo, acc, query, mixed, rh, rf, ry, wkv,
+    qs, qr, os_, or_, hs, hr, fs, fr, ys, yr, tsem, ksem, lsem,
+):
+    z, ylo, yhi, x, c = where_am_i()
+    near = neighbours()
+    count = tok.shape[1]
+    chunk = tok.shape[2]
+    half = count // 2
+    scale = 128 ** -0.5
+
+    own_q = pltpu.make_async_copy(wq_hbm, wq.at[0, 0], lsem.at[0])
+    own_o = pltpu.make_async_copy(wo_hbm, wo.at[0, 0], lsem.at[1])
+    own_q.start()
+
+    barrier = pltpu.get_barrier_semaphore()
+    for way in ("xp", "xm", "y", "sib", "zp", "zm", "yl"):
+        pl.semaphore_signal(barrier, inc=1, device_id=near[way], device_id_type=MESH)
+    pl.semaphore_wait(barrier, 7)
+
+    gq = Gather(wq, CUT_Q, qs, qr, near)
+    go = Gather(wo, CUT_O, os_, or_, near)
+    own_q.wait()
+    gq.start(FIRST)
+
+    def tok_copy(r):
+        return pltpu.make_async_copy(tok_hbm.at[:, pl.ds(r * chunk, chunk)], tok.at[r], tsem.at[r])
+
+    def kv_copy(r, slot):
+        return pltpu.make_async_copy(wkv_hbm.at[pl.ds(r * chunk, chunk)], wkv.at[slot], ksem.at[slot])
+
+    kv_copy(0, 0).start()
+    for r in range(16):
+        tok_copy(r).start()
+    own_o.start()
+    acc[...] = jnp.zeros_like(acc)
+
+    @pl.loop(0, 16)
+    def _(r):
+        slot = r % 2
+
+        @pl.when(r < 15)
+        def _():
+            kv_copy(r + 1, 1 - slot).start()
+
+        tok_copy(r).wait()
+        kv_copy(r, slot).wait()
+        acc[:, 0:256] += jnp.dot(tok[r], wkv[slot], preferred_element_type=F32)
+
+    kv_ref[...] = acc[:, 0:256].astype(BF16)
+    acc[...] = jnp.zeros_like(acc)
+
+    def place(unit):
+        (dx, dy), part = unit
+        return (x + dx) % 4, (yhi + dy) % 2
+
+    def query_unit(unit):
+        (dx, dy), part = unit
+        slot = dy * 4 + dx
+        xs, yhs = place(unit)
+        start, size = row_range(part, CUT_Q, chunk)
+        gq.shared(unit)
+
+        @pl.loop(0, 8)
+        def _(j):
+            lane = j // 4
+            cols = pl.ds(pl.multiple_of((j % 4) * 256, 256), 256)
+            r = yhs * 8 + xs * 2 + c + lane * (1 - 2 * c)
+            acc[:, cols] += jnp.dot(
+                tok[r, :, start:start + size],
+                wq[lane, slot, start:start + size, cols],
+                preferred_element_type=F32,
+            )
+
+    query_unit(UNITS[0])
+    query_unit(UNITS[1])
+    waiting = []
+    for k in range(len(EVENTS)):
+        gq.event(k)
+        if k == 4:
+            own_o.wait()
+            go.start(FIRST)
+        for unit in waiting:
+            query_unit(unit)
+        waiting = EVENTS[k][2]
+    for unit in waiting:
+        query_unit(unit)
+    query[...] = acc[...].astype(BF16)
+
+    for b in range(4):
+        first = max(b - 1, 0) * 128
+        rows = slice(b * 128, b * 128 + 128)
+        q8 = jnp.concatenate([query[rows, h * 128:h * 128 + 128] for h in range(8)], axis=0)
+        keys = kv_ref[first:first + 256, 0:128]
+        values = kv_ref[first:first + 256, 128:256]
+        s = lax.dot_general(q8, keys, (((1,), (1,)), ((), ())), preferred_element_type=F32) * scale
+        s = (s.reshape(8, 128, 256) + bias_ref[b][None]).reshape(1024, 256)
+        e = jnp.exp(s - jnp.max(s, axis=1, keepdims=True))
+        total = jnp.sum(e, axis=1, keepdims=True)
+        o = jnp.dot(e.astype(BF16), values, preferred_element_type=F32) / total
+        o = o.astype(BF16)
+        for h in range(8):
+            mixed[rows, h * 128:h * 128 + 128] = o[h * 128:h * 128 + 128]
+        if b < 3:
+            go.event(b)
+
+    def role(unit):
+        xs, yhs = place(unit)
+        return (z + 4 - (yhs * 2 + xs // 2)) % 4, xs % 2
+
+    def cols_of(unit):
+        start, size = row_range(unit[1], CUT_O, chunk)
+        return pl.ds(start, size)
+
+    def slot_of(unit):
+        return unit[0][1] * 4 + unit[0][0]
+
+    def half_copy(k, which):
+        unit = UNITS[k]
+        return pltpu.make_async_remote_copy(
+            src_ref=tok.at[pl.ds(2 * slot_of(unit), 2), pl.ds(which * half, half), cols_of(unit)],
+            dst_ref=rh.at[slot_of(unit), :, :, cols_of(unit)],
+            send_sem=hs.at[k, which],
+            recv_sem=hr.at[k, which],
+            device_id=near["zm" if which else "zp"],
+            device_id_type=MESH,
+        )
+
+    def full_copy(k, which):
+        unit = UNITS[k]
+        return pltpu.make_async_remote_copy(
+            src_ref=tok.at[pl.ds(2 * slot_of(unit), 2), :, cols_of(unit)],
+            dst_ref=rf.at[role(unit)[1], which, :, :, cols_of(unit)],
+            send_sem=fs.at[k],
+            recv_sem=fr.at[k, which],
+            device_id=near["zm" if which else "zp"],
+            device_id_type=MESH,
+        )
+
+    def y_copy(k):
+        unit = UNITS[k]
+        return pltpu.make_async_remote_copy(
+            src_ref=tok.at[pl.ds(2 * slot_of(unit), 2), :, cols_of(unit)],
+            dst_ref=ry.at[:, :, cols_of(unit)],
+            send_sem=ys.at[k],
+            recv_sem=yr.at[k],
+            device_id=near["yl"],
+            device_id_type=MESH,
+        )
+
+    def partial_unit(k):
+        unit = UNITS[k]
+        slot = slot_of(unit)
+        start, size = row_range(unit[1], CUT_O, chunk)
+        go.shared(unit)
+
+        @pl.loop(0, 2)
+        def _(lane):
+            tok[2 * slot + lane, :, start:start + size] = lax.dot_general(
+                mixed[...],
+                wo[lane, slot, start:start + size, :],
+                (((1,), (1,)), ((), ())),
+                preferred_element_type=F32,
+            ).astype(BF16)
+
+        dz, _ = role(unit)
+
+        @pl.when(dz == 2)
+        def _():
+            half_copy(k, 0).start()
+            half_copy(k, 1).start()
+
+    STEP = 64
+
+    def pass_on(k):
+        unit = UNITS[k]
+        slot = slot_of(unit)
+        start, size = row_range(unit[1], CUT_O, chunk)
+        dz, _ = role(unit)
+        for which in range(2):
+
+            @pl.when(dz == (1 if which else 3))
+            def _():
+                half_copy(k, which).wait_recv()
+
+                @pl.loop(0, 2 * (half // STEP))
+                def _(j):
+                    lane = j // (half // STEP)
+                    i = pl.multiple_of((j % (half // STEP)) * STEP, STEP)
+                    there = tok[2 * slot + lane, pl.ds(i + which * half, STEP), start:start + size]
+                    more = rh[slot, lane, pl.ds(i, STEP), start:start + size]
+                    tok[2 * slot + lane, pl.ds(i + which * half, STEP), start:start + size] = (
+                        there.astype(F32) + more.astype(F32)
+                    ).astype(BF16)
+
+                full_copy(k, which).start()
+
+    def collect(k):
+        unit = UNITS[k]
+        slot = slot_of(unit)
+        start, size = row_range(unit[1], CUT_O, chunk)
+        dz, ylos = role(unit)
+
+        @pl.when(dz == 0)
+        def _():
+            full_copy(k, 0).wait_recv()
+            full_copy(k, 1).wait_recv()
+
+            def summed(j):
+                lane = j // (count // STEP)
+                i = pl.multiple_of((j % (count // STEP)) * STEP, STEP)
+                rows = pl.ds(i, STEP)
+                total = tok[2 * slot + lane, rows, start:start + size].astype(F32)
+                total += rf[ylos, 0, lane, rows, start:start + size].astype(F32)
+                total += rf[ylos, 1, lane, rows, start:start + size].astype(F32)
+                return lane, rows, total
+
+            @pl.when(ylos == ylo)
+            def _():
+                @pl.loop(0, 2 * (count // STEP))
+                def _(j):
+                    lane, rows, total = summed(j)
+                    acc[rows, pl.ds(pl.multiple_of(lane * chunk + start, 128), size)] = total
+
+            @pl.when(ylos != ylo)
+            def _():
+                @pl.loop(0, 2 * (count // STEP))
+                def _(j):
+                    lane, rows, total = summed(j)
+                    tok[2 * slot + lane, rows, start:start + size] = total.astype(BF16)
+
+                y_copy(k).start()
+
+    def deliver(k):
+        unit = UNITS[k]
+        start, size = row_range(unit[1], CUT_O, chunk)
+        dz, ylos = role(unit)
+
+        @pl.when((dz == 0) & (ylos == ylo))
+        def _():
+            y_copy(k).wait_recv()
+
+            @pl.loop(0, 2 * (count // STEP))
+            def _(j):
+                lane = j // (count // STEP)
+                rows = pl.ds(pl.multiple_of((j % (count // STEP)) * STEP, STEP), STEP)
+                total = acc[rows, pl.ds(pl.multiple_of(lane * chunk + start, 128), size)]
+                total += ry[lane, rows, start:start + size].astype(F32)
+                place_ = (c + lane * (1 - 2 * c)) * chunk + start
+                out_ref[rows, pl.ds(pl.multiple_of(place_, 128), size)] = total.astype(BF16)
+
+    steps = [(None, [0, 1])]
+    at = 2
+    for k in range(len(EVENTS)):
+        steps.append((k, list(range(at, at + len(EVENTS[k][2])))))
+        at += len(EVENTS[k][2])
+    done = [0]
+
+    def advance(k):
+        partial_unit(k)
+        if k >= LAG1:
+            pass_on(k - LAG1)
+        if k >= LAG2:
+            collect(k - LAG2)
+
+    pending = [0, 1] + steps[1][1] + steps[2][1]
+    for u in pending:
+        advance(u)
+    pending = list(steps[3][1])
+    for k in range(3, len(EVENTS)):
+        go.event(k)
+        for u in pending:
+            advance(u)
+        pending = list(steps[k + 1][1])
+    for u in pending:
+        advance(u)
+    n = len(UNITS)
+    for k in range(n - LAG1, n):
+        pass_on(k)
+    for k in range(n - LAG2, n):
+        collect(k)
+    for k in range(n):
+        deliver(k)
+
+    gq.finish()
+    go.finish()
+    for k in range(n):
+        dz, ylos = role(UNITS[k])
+
+        @pl.when(dz == 2)
+        def _():
+            half_copy(k, 0).wait_send()
+            half_copy(k, 1).wait_send()
+
+        for which in range(2):
+
+            @pl.when(dz == (1 if which else 3))
+            def _():
+                full_copy(k, which).wait_send()
+
+        @pl.when((dz == 0) & (ylos != ylo))
+        def _():
+            y_copy(k).wait_send()
+
+
+def layer(tokens, wq, wkv, wo, bias):
+    count, model = tokens.shape
+    rows, cols = wq.shape
+    any_ = pl.BlockSpec(memory_space=pl.ANY)
+    vmem = pl.BlockSpec(memory_space=pltpu.VMEM)
+    dma = pltpu.SemaphoreType.DMA
+    n = len(UNITS)
+    return pl.pallas_call(
+        layer_kernel,
+        name="layer",
+        out_shape=(
+            jax.ShapeDtypeStruct((count, cols), BF16),
+            jax.ShapeDtypeStruct((count, 256), BF16),
+        ),
+        in_specs=[any_, any_, any_, any_, vmem],
+        out_specs=(vmem, vmem),
+        scratch_shapes=[
+            pltpu.VMEM((16, count, 512), BF16),
+            pltpu.VMEM((2, 8, rows, cols), BF16),
+            pltpu.VMEM((2, 8, rows, cols), BF16),
+            pltpu.VMEM((count, cols), F32),
+            pltpu.VMEM((count, cols), BF16),
+            pltpu.VMEM((count, cols), BF16),
+            pltpu.VMEM((8, 2, count // 2, 512), BF16),
+            pltpu.VMEM((2, 2, 2, count, 512), BF16),
+            pltpu.VMEM((2, count, 512), BF16),
+            pltpu.VMEM((2, 512, 256), BF16),
+            dma((N_MOVES,)), dma((N_MOVES,)), dma((N_MOVES,)), dma((N_MOVES,)),
+            dma((n, 2)), dma((n, 2)), dma((n,)), dma((n, 2)), dma((n,)), dma((n,)),
+            dma((16,)), dma((2,)), dma((2,)),
+        ],
+        compiler_params=pltpu.CompilerParams(
+            collective_id=0, has_side_effects=True, vmem_limit_bytes=63 * 2**20
+        ),
+    )(tokens, wq, wkv, wo, bias)
 
 
 def segment_ids(lens, count):
@@ -12,26 +479,16 @@
     return jnp.sum((position[:, None] >= ends[None, :]).astype(jnp.int32), axis=1)
 
 
-def prefill_attend(query, keyval, lens):
-    count, heads = (keyval.shape[0], keyval.shape[1])
-    width = keyval.shape[2] // 2
-    group = query.shape[2] // width
-    scale = width ** (-0.5)
+def window_bias(lens, count):
     seg = segment_ids(lens, count)
-    position = jnp.arange(count, dtype=jnp.int32)
-    allowed = (seg[:, None] == seg[None, :]) & (position[None, :] <= position[:, None])
-    q_four = query.reshape(count, heads, group, width)
-    keys = keyval[:, :, :width]
-    values = keyval[:, :, width:]
-    scores = jnp.einsum("ihgd,jhd->hgij", q_four, keys, preferred_element_type=jnp.float32) * scale
-    scores = jnp.where(allowed[None, None], scores, NEG)
-    top = jnp.max(scores, axis=-1, keepdims=True)
-    expo = jnp.exp(scores - top)
-    total = jnp.sum(expo, axis=-1)
-    weights = expo.astype(jnp.bfloat16)
-    acc = jnp.einsum("hgij,jhd->ihgd", weights, values, preferred_element_type=jnp.float32)
-    mixed = acc / jnp.transpose(total, (2, 0, 1))[..., None]
-    return mixed.astype(jnp.bfloat16).reshape(count, heads * group * width)
+    out = []
+    for b in range(count // 128):
+        first = max(b - 1, 0) * 128
+        rows = jnp.arange(b * 128, b * 128 + 128, dtype=jnp.int32)
+        cols = jnp.arange(first, first + 256, dtype=jnp.int32)
+        ok = (seg[b * 128:b * 128 + 128, None] == seg[None, first:first + 256]) & (cols[None, :] <= rows[:, None])
+        out.append(jnp.where(ok, 0.0, NEG).astype(F32))
+    return jnp.stack(out)
 
 
 def decode_attend(query, cache, fresh, stretch, cache_rows, stretch_rows):
@@ -82,33 +539,18 @@
 def local(
     tokens, w_query, w_keyval, output_weight, cache, fresh, decode_query, cache_len, new_len, route
 ):
-    f32 = jnp.float32
     count, model = tokens.shape
     heads = w_keyval.shape[1]
     width = w_keyval.shape[2] // 2
     groups, slots = (route.shape[0], route.shape[1])
     my_group = lax.axis_index("req")
-    qcols = w_query.shape[1] * w_query.shape[2]
-    piece = lax.all_gather(w_query, "req", axis=0, tiled=True)
-    query = jnp.dot(
-        tokens, piece.reshape(piece.shape[0], qcols), preferred_element_type=f32
-    ).astype(jnp.bfloat16)
-    keyval = jnp.dot(tokens, w_keyval.reshape(model, -1), preferred_element_type=f32).astype(
-        jnp.bfloat16
-    )
     my_lens = lax.dynamic_index_in_dim(new_len, my_group, 0, keepdims=False)
-    mixed = prefill_attend(
-        query.reshape(count, heads, -1), keyval.reshape(count, heads, 2 * width), my_lens
-    )
-    piece = lax.all_gather(output_weight, "req", axis=0, tiled=True)
-    partial_terms = lax.dot_general(
-        mixed,
-        piece.reshape(piece.shape[0], qcols),
-        (((1,), (1,)), ((), ())),
-        preferred_element_type=f32,
-    )
-    prefill_out = lax.psum_scatter(partial_terms, "tp", scatter_dimension=1, tiled=True).astype(
-        jnp.bfloat16
+    prefill_out, keyval = layer(
+        tokens,
+        w_query.reshape(w_query.shape[0], -1),
+        w_keyval.reshape(model, -1),
+        output_weight.reshape(output_weight.shape[0], -1),
+        window_bias(my_lens, count),
     )
     offsets = jnp.cumsum(my_lens) - my_lens
     my_route = lax.dynamic_index_in_dim(route, my_group, 0, keepdims=False)

time: 590 us -> 300 us (0.51)
  waiting for transfers between devices: 505 us -> 4.67 us
  Pallas kernels: 0 us -> 238 us
  matrix products: 50.1 us -> 8.46 us
  starting transfers between devices: 5.73 us -> 33.4 us
  between operations: 13.9 us -> 0.86 us
    reduce_scatter x1 -> x0, waiting for transfers between devices: 305 us -> none  [local(): lax.psum_scatter(partial_terms, 'tp', scatter_dimension=1, tiled=True)]
    pallas_call x0 -> x1, Pallas kernels: none -> 238 us  [layer(): pl.pallas_call(layer_kernel, name='layer', out_shape=(jax.ShapeDtypeStruc...]
    all_gather x2 -> x0, waiting for transfers between devices: 194 us -> none  [the longest x1 104 us: local(): piece = lax.all_gather(w_query, 'req', axis=0, tiled=True)]
    dot_general x5 -> x0, matrix products: 41.6 us -> none  [the longest x1 15.8 us: local(): lax.dot_general(mixed, piece.reshape(piece.shape[0], qcols), (((1,), (1,)...]
    all_to_all x1, starting transfers between devices: 5.62 us -> 33.4 us  [local(): lax.all_to_all(outgoing, 'req', split_axis=0, concat_axis=0, tiled=True)]
  transfers between devices with their start and end apart: 4 -> 1, of which waited for: 4 -> 1; matrix products, arithmetic and copies ran while one was open for 8% -> 2% of each run, Pallas kernels for 0% -> 0%
where the time goes in v1:
time: 300 us; the launch traced here: 297 us
  Pallas kernels  238 us (79%)
  starting transfers between devices  33.4 us (11%)
  local copies, waits for them, and re-layouts  8.59 us (3%)
  matrix products  8.46 us (3%)
  waiting for transfers between devices  4.67 us (2%)
  other arithmetic  3.66 us (1%)
    pallas_call x1, Pallas kernels, layer(): pl.pallas_call(layer_kernel, name='layer', out_shape=(jax.ShapeDtypeStruc...  238 us
    all_to_all x1, starting transfers between devices, local(): lax.all_to_all(outgoing, 'req', split_axis=0, concat_axis=0, tiled=True)  33.4 us
  transfers between devices with their start and end apart: 1, of which 1 were waited for; matrix products, arithmetic and copies ran while one was open for 2% of the time, Pallas kernels for 0%

profile of v1, /device:TPU:24, one launch (start us, length us, event | category | flops | bytes accessed | tf_op | source)
XLA Modules:
  0.0 297.3 jit_solution(7728462337681239280)
XLA Ops:
  0.6 0.7 fusion.40
  1.5 0.1 reduce.12
  1.7 0.7 fusion.39
  2.4 0.1 select_reduce_fusion
  2.7 0.1 and_select_fusion.1
  2.8 0.2 fusion.29
  3.0 0.8 pad_maximum_fusion.bias_ref
  3.8 237.7 %layer.1 = (bf16[512,1024]{1,0:T(8,128)(2,1)}, bf16[512,256]{1,0:T(8,128)(2,1)}) custom-call(bf16[512,8192]{1,0:T(8,128)(2,1)} %tok_hbm.1, bf16[512,1024]{1,0:T(8,128)(2,1)} %bitcast.113, bf16[8192,256]{1,0:T(8,128)(2,1)} %bitcast.112, bf16[512,1024]{1,0:T(8,128)(2,1)} %bitcast.114, f32[4,128,256]{2,1,0:T(8,128)} %pad_maximum_fusion.bias_ref), custom_call_target="tpu_custom_call" | custom-call | tf_op jit(solution)/shard_map/layer/pallas_call | solution.py:446
  241.5 1.0 concatenate.3
  242.5 5.0 %gather_fusion = bf16[1024,256]{1,0:T(8,128)(2,1)} fusion(bf16[576,256]{1,0:T(8,128)(2,1)S(1)} %concatenate.3, s32[1024]{0:T(1024)S(1)} %broadcast_clamp_fusion), kind=kCustom, calls=%fused_computation | custom fusion | bytes 1052672 | tf_op jit(solution)/shard_map/gather | solution.py:564
  247.5 33.4 %all-to-all-start = ((bf16[16,64,256]{2,1,0:T(8,128)(2,1)}), bf16[16,64,256]{2,1,0:T(8,128)(2,1)S(1)}, u32[]{:S(2)}, u32[]{:S(2)}) async-start(bf16[16,64,256]{2,1,0:T(8,128)(2,1)} %bitcast.10), calls=%async_computation | async-start | bytes 1048576 | tf_op jit(solution)/shard_map/all_to_all | solution.py:565
  281.0 0.1 select_reduce_fusion.1
  281.2 0.7 fusion.46
  282.0 3.7 %fusion.6 = (f32[16,4,8]{2,1,0:T(4,128)S(1)}, f32[16,4,8,1024]{3,2,1,0:T(8,128)S(1)}) fusion(pred[16,1024]{1,0:T(8,128)(4,1)S(1)} %iota_compare_fusion.2, bf16[2,16,1024,128]{3,2,1,0:T(8,128)(2,1)} %param.14, bf16[4,16,8,128]{3,2,1,0:T(8,128)(2,1)S(1)} %bitcast.122), kind=kOutput, calls=%fused_computation.9 | convolution fusion | flops 135790080 | bytes 6440960 | tf_op jit(solution)/shard_map/trhgd,rchd->rhtgc/dot_general | solution.py:510
  285.8 4.7 %all-to-all-done = bf16[16,64,256]{2,1,0:T(8,128)(2,1)S(1)} async-done(((bf16[16,64,256]{2,1,0:T(8,128)(2,1)}), bf16[16,64,256]{2,1,0:T(8,128)(2,1)S(1)}, u32[]{:S(2)}, u32[]{:S(2)}) %all-to-all-start) | async-done | bytes 524320 | tf_op jit(solution)/shard_map/all_to_all | solution.py:565
  290.4 0.3 fusion.47
  290.8 0.6 fusion.7
  291.4 3.2 %fusion.9 = f32[16,128,4,8]{1,3,2,0:T(8,128)S(1)} fusion(bf16[2,16,1024,128]{3,2,1,0:T(8,128)(2,1)} %param.14, f32[16,4,8,1024]{3,2,1,0:T(8,128)S(1)} %get-tuple-element.26, f32[16,4,8]{2,1,0:T(4,128)S(1)} %bitcast.116, pred[16,1024]{1,0:T(8,128)(4,1)S(1)} %iota_compare_fusion.2), kind=kOutput, calls=%fused_computation.12 | convolution fusion | flops 136314880 | bytes 6572032 | tf_op jit(solution)/shard_map/rhtgc,rchd->trhgd/dot_general | solution.py:526
  294.6 0.3 fusion.24
  294.9 0.1 fusion.32
  295.1 0.2 convolution_bitcast_fusion
  295.3 0.3 fusion.18
  295.6 0.7 copy.32
  296.3 1.0 copy.61
  (33 shorter events, 0.7 us)
Async XLA Ops:
  242.5 38.5 %copy-start.3 = (s32[16,16]{1,0:T(8,128)S(1)}, s32[16,16]{1,0:T(8,128)}, u32[]{:S(2)}) copy-start(s32[16,16]{1,0:T(8,128)} %param.18) | copy-start | bytes 3076
  242.5 38.5 %copy-start.4 = (s32[16,16]{1,0:T(8,128)S(1)}, s32[16,16]{1,0:T(8,128)}, u32[]{:S(2)}) copy-start(s32[16,16]{1,0:T(8,128)} %param.19) | copy-start | bytes 3076
  242.5 38.6 %copy-start.1 = (bf16[4,16,1024]{2,1,0:T(8,128)(2,1)S(1)}, bf16[4,16,1024]{2,1,0:T(8,128)(2,1)}, u32[]{:S(2)}) copy-start(bf16[4,16,1024]{2,1,0:T(8,128)(2,1)} %param.16) | copy-start | bytes 393220
  242.5 38.6 %copy-start.5 = (s32[1,16]{1,0:T(1,128)S(1)}, s32[1,16]{1,0:T(1,128)}, u32[]{:S(2)}) copy-start(s32[1,16]{1,0:T(1,128)} %param.17) | copy-start | bytes 196
  242.5 38.7 %copy-start.2 = (bf16[2,4,16,128]{3,2,1,0:T(8,128)(2,1)S(1)}, bf16[2,4,16,128]{3,2,1,0:T(8,128)(2,1)}, u32[]{:S(2)}) copy-start(bf16[2,4,16,128]{3,2,1,0:T(8,128)(2,1)} %param.15) | copy-start | bytes 98308
  247.5 42.9 %all-to-all-start = ((bf16[16,64,256]{2,1,0:T(8,128)(2,1)}), bf16[16,64,256]{2,1,0:T(8,128)(2,1)S(1)}, u32[]{:S(2)}, u32[]{:S(2)}) async-start(bf16[16,64,256]{2,1,0:T(8,128)(2,1)} %bitcast.10), calls=%async_computation | async-start | bytes 1048576 | tf_op jit(solution)/shard_map/all_to_all | solution.py:565
  294.6 1.7 copy-start

commit v2 on v1

v2 whole, which is shorter than its diff:
```python
import functools

import jax
import jax.numpy as jnp
from jax import lax
from jax.experimental import pallas as pl
from jax.experimental.pallas import tpu as pltpu
from jax.sharding import PartitionSpec as P

NEG = -1e30
MESH = pl.DeviceIdType.MESH
F32 = jnp.float32
BF16 = jnp.bfloat16

CUT_Q = 384
START_O = 3

MOVES_A = {
    "yA": ((0, 0), "A", (0, 1), "y"),
    "xpA": ((0, 0), "A", (3, 0), "xp"),
    "xmA": ((0, 0), "A", (1, 0), "xm"),
    "xpC": ((0, 1), "A", (3, 1), "xp"),
    "xmC": ((0, 1), "A", (1, 1), "xm"),
    "fpA": ((3, 0), "A0", (2, 0), "xp"),
    "fmA": ((1, 0), "A1", (2, 0), "xm"),
    "fpC": ((3, 1), "A0", (2, 1), "xp"),
    "fmC": ((1, 1), "A1", (2, 1), "xm"),
}
MOVES_B = {
    "xpB": ((0, 0), "B", (3, 0), "xp"),
    "xmB": ((0, 0), "B", (1, 0), "xm"),
    "fpB": ((3, 0), "B0", (2, 0), "xp"),
    "fmB": ((1, 0), "B1", (2, 0), "xm"),
    "yB0": ((0, 0), "B", (0, 1), "y"),
    "yBm": ((3, 0), "B", (3, 1), "y"),
    "yBp": ((1, 0), "B", (1, 1), "y"),
    "yB2p": ((2, 0), "B0", (2, 1), "y"),
    "yB2m": ((2, 0), "B1", (2, 1), "y"),
}
SLOTS = [(dx, dy) for dy in range(2) for dx in range(4)]


def shares(units):
    return {"s%d%d%s" % (slot + (part,)): (slot, part, slot, "sib") for slot, part in units}


FIRST_Q = ["yA", "xpA", "xmA", "s00A", "xpB", "xmB", "yB0", "s00B"]
EVENTS_Q = [
    (["yA"], ["xpC", "xmC", "s01A"], [((0, 1), "A")]),
    (["xpA", "xmA"], ["fpA", "fmA", "s30A", "s10A"], [((3, 0), "A"), ((1, 0), "A")]),
    (["xpB", "xmB"], ["fpB", "fmB", "yBm", "yBp", "s30B", "s10B"], [((3, 0), "B"), ((1, 0), "B")]),
    (["xpC", "xmC"], ["fpC", "fmC", "s31A", "s11A"], [((3, 1), "A"), ((1, 1), "A")]),
    (["fpA", "fmA"], ["s20A"], [((2, 0), "A")]),
    (["fpB", "fmB"], ["yB2p", "yB2m", "s20B"], [((2, 0), "B")]),
    (["yB0"], ["s01B"], [((0, 1), "B")]),
    (["yBm", "yBp"], ["s31B", "s11B"], [((3, 1), "B"), ((1, 1), "B")]),
    (["fpC", "fmC"], ["s21A"], [((2, 1), "A")]),
    (["yB2p", "yB2m"], ["s21B"], [((2, 1), "B")]),
]
UNITS_Q = [((0, 0), "A"), ((0, 0), "B")] + [u for e in EVENTS_Q for u in e[2]]
MOVES_Q = {**MOVES_A, **MOVES_B, **shares(UNITS_Q)}
FIRST_O = ["xpA", "xmA", "yA", "s00A"]
EVENTS_O = [
    (["yA"], ["xpC", "xmC", "s01A"], [((0, 1), "A")]),
    (["xpA", "xmA"], ["fpA", "fmA", "s30A", "s10A"], [((3, 0), "A"), ((1, 0), "A")]),
    (["xpC", "xmC"], ["fpC", "fmC", "s31A", "s11A"], [((3, 1), "A"), ((1, 1), "A")]),
    (["fpA"], ["s20A0"], [((2, 0), "A0")]),
    (["fmA"], ["s20A1"], [((2, 0), "A1")]),
    (["fpC"], ["s21A0"], [((2, 1), "A0")]),
    (["fmC"], ["s21A1"], [((2, 1), "A1")]),
]
UNITS_O = [((0, 0), "A")] + [u for e in EVENTS_O for u in e[2]]
HALVES = [(u, r, 256) for r in (0, 256) for u in UNITS_O[:4]]
ITEMS = HALVES + [(u, 0, 512) for u in UNITS_O[4:8]] + [(u, r, 256) for u in UNITS_O[8:] for r in (0, 256)]
PLAN = (
    [("mixed", 0), ("part", 0), ("part", 1), ("event", 1), ("part", 2), ("part", 3), ("mixed", 1)]
    + [("part", i) for i in range(4, 8)]
    + [("event", 2), ("collect", 0), ("collect", 1), ("part", 8), ("part", 9)]
    + [("collect", i) for i in range(2, 8)]
    + [("event", 3), ("event", 4), ("part", 10), ("part", 11), ("collect", 8), ("collect", 9)]
    + [("event", 5), ("part", 12), ("part", 13), ("event", 6), ("part", 14), ("part", 15)]
    + [("collect", i) for i in range(10, 16)]
)
MOVES_O = {**MOVES_A, **shares(UNITS_O)}


def where_am_i():
    tp = lax.axis_index("tp")
    req = lax.axis_index("req")
    return tp // 2, tp % 2, req // 8, (req // 2) % 4, req % 2


def neighbours():
    z, ylo, yhi, x, c = where_am_i()
    tp = z * 2 + ylo
    req = yhi * 8 + x * 2 + c
    return {
        "xp": (tp, yhi * 8 + ((x + 1) % 4) * 2 + c),
        "xm": (tp, yhi * 8 + ((x + 3) % 4) * 2 + c),
        "y": (tp, (1 - yhi) * 8 + x * 2 + c),
        "sib": (tp, yhi * 8 + x * 2 + (1 - c)),
        "z1": (((z + 1) % 4) * 2 + ylo, req),
        "z2": (((z + 2) % 4) * 2 + ylo, req),
        "z3": (((z + 3) % 4) * 2 + ylo, req),
        "yl": (z * 2 + (1 - ylo), req),
    }


def row_range(part, cut, rows):
    rest = rows - cut
    return {
        "A": (0, cut),
        "A0": (0, cut // 2),
        "A1": (cut // 2, cut // 2),
        "B": (cut, rest),
        "B0": (cut, rest // 2),
        "B1": (cut + rest // 2, rest // 2),
    }[part]


class Gather:
    def __init__(self, view, moves, events, rows, cut, send, recv, near):
        self.view, self.moves, self.events = view, moves, events
        self.rows, self.cut, self.send, self.recv, self.near = rows, cut, send, recv, near
        self.index = {name: i for i, name in enumerate(moves)}

    def copy(self, name):
        src, part, dst, way = self.moves[name]
        start, size = row_range(part, self.cut, self.rows)
        lane = 1 if way == "sib" else 0
        i = self.index[name]
        return pltpu.make_async_remote_copy(
            src_ref=self.view(0, src[1] * 4 + src[0], pl.ds(start, size)),
            dst_ref=self.view(lane, dst[1] * 4 + dst[0], pl.ds(start, size)),
            send_sem=self.send.at[i],
            recv_sem=self.recv.at[i],
            device_id=self.near[way],
            device_id_type=MESH,
        )

    def start(self, names):
        for name in names:
            self.copy(name).start()

    def event(self, k):
        waits, starts, _ = self.events[k]
        for name in waits:
            self.copy(name).wait_recv()
        self.start(starts)

    def shared(self, unit):
        (dx, dy), part = unit
        self.copy("s%d%d%s" % (dx, dy, part)).wait_recv()

    def finish(self):
        for name in self.moves:
            self.copy(name).wait_send()


def layer_kernel(
    tok_hbm, wq_hbm, wkv_hbm, wo_hbm, bias_ref,
    out_ref, kv_ref,
    tok, wq, wo, acc, query, mixed, rf, wkv,
    qs, qr, os_, or_, ms, mr, ps, pr, fs, fr, ys, yr, tsem, ksem, lsem,
):
    z, ylo, yhi, x, c = where_am_i()
    near = neighbours()
    count = tok.shape[1]
    chunk = tok.shape[2]
    half = chunk // 2
    scale = 128 ** -0.5

    own_q = pltpu.make_async_copy(wq_hbm, wq.at[0, 0], lsem.at[0])
    own_o = pltpu.make_async_copy(
        wo_hbm.at[pl.ds(pl.multiple_of(ylo * half, half), half)], wo.at[0, 0, 0], lsem.at[1]
    )
    own_q.start()

    barrier = pltpu.get_barrier_semaphore()
    for way in near:
        pl.semaphore_signal(barrier, inc=1, device_id=near[way], device_id_type=MESH)
    pl.semaphore_wait(barrier, len(near))

    gq = Gather(lambda lane, slot, rows: wq.at[lane, slot, rows], MOVES_Q, EVENTS_Q, chunk, CUT_Q, qs, qr, near)
    go = Gather(lambda lane, slot, rows: wo.at[lane, slot, :, rows], MOVES_O, EVENTS_O, half, half, os_, or_, near)
    swap_o = pltpu.make_async_remote_copy(
        src_ref=wo_hbm.at[pl.ds(pl.multiple_of((1 - ylo) * half, half), half)],
        dst_ref=wo.at[0, 0, 1],
        send_sem=ps.at[0],
        recv_sem=pr.at[0],
        device_id=near["yl"],
        device_id_type=MESH,
    )
    own_q.wait()
    gq.start(FIRST_Q)

    def tok_copy(r):
        return pltpu.make_async_copy(tok_hbm.at[:, pl.ds(r * chunk, chunk)], tok.at[r], tsem.at[r])

    def kv_copy(r, slot):
        return pltpu.make_async_copy(wkv_hbm.at[pl.ds(r * chunk, chunk)], wkv.at[slot], ksem.at[slot])

    kv_copy(0, 0).start()
    for r in range(16):
        tok_copy(r).start()
    own_o.start()
    acc[...] = jnp.zeros_like(acc)

    @pl.loop(0, 16)
    def _(r):
        slot = r % 2

        @pl.when(r < 15)
        def _():
            kv_copy(r + 1, 1 - slot).start()

        tok_copy(r).wait()
        kv_copy(r, slot).wait()
        acc[:, 0:256] += jnp.dot(tok[r], wkv[slot], preferred_element_type=F32)

    kv_ref[...] = acc[:, 0:256].astype(BF16)
    acc[...] = jnp.zeros_like(acc)

    def place(unit):
        (dx, dy), part = unit
        return (x + dx) % 4, (yhi + dy) % 2

    def slot_of(unit):
        return unit[0][1] * 4 + unit[0][0]

    def query_unit(unit):
        slot = slot_of(unit)
        xs, yhs = place(unit)
        start, size = row_range(unit[1], CUT_Q, chunk)
        gq.shared(unit)

        @pl.loop(0, 8)
        def _(j):
            lane = j // 4
            cols = pl.ds(pl.multiple_of((j % 4) * 256, 256), 256)
            r = yhs * 8 + xs * 2 + c + lane * (1 - 2 * c)
            acc[:, cols] += jnp.dot(
                tok[r, :, start:start + size],
                wq[lane, slot, start:start + size, cols],
                preferred_element_type=F32,
            )

    query_unit(UNITS_Q[0])
    query_unit(UNITS_Q[1])
    waiting = []
    for k in range(len(EVENTS_Q)):
        gq.event(k)
        if k == 1:
            swap_o.start()
        if k == START_O:
            own_o.wait()
            swap_o.wait_recv()
            go.start(FIRST_O)
        for unit in waiting:
            query_unit(unit)
        waiting = EVENTS_Q[k][2]
    for unit in waiting:
        query_unit(unit)
    query[...] = acc[...].astype(BF16)

    def swap_mixed(b):
        rows = pl.ds(b * 256, 256)
        return pltpu.make_async_remote_copy(
            src_ref=mixed.at[0, rows],
            dst_ref=mixed.at[1, rows],
            send_sem=ms.at[b],
            recv_sem=mr.at[b],
            device_id=near["yl"],
            device_id_type=MESH,
        )

    for b in range(4):
        first = max(b - 1, 0) * 128
        rows = slice(b * 128, b * 128 + 128)
        q8 = jnp.concatenate([query[rows, h * 128:h * 128 + 128] for h in range(8)], axis=0)
        keys = kv_ref[first:first + 256, 0:128]
        values = kv_ref[first:first + 256, 128:256]
        s = lax.dot_general(q8, keys, (((1,), (1,)), ((), ())), preferred_element_type=F32) * scale
        s = (s.reshape(8, 128, 256) + bias_ref[b][None]).reshape(1024, 256)
        e = jnp.exp(s - jnp.max(s, axis=1, keepdims=True))
        total = jnp.sum(e, axis=1, keepdims=True)
        o = jnp.dot(e.astype(BF16), values, preferred_element_type=F32) / total
        o = o.astype(BF16)
        for h in range(8):
            mixed[0, rows, h * 128:h * 128 + 128] = o[h * 128:h * 128 + 128]
        if b % 2 == 1:
            swap_mixed(b // 2).start()
        if b == 1:
            go.event(0)

    def role(unit):
        xs, yhs = place(unit)
        zs = yhs * 2 + xs // 2
        return (z + 4 - zs) % 4, zs, xs % 2

    def z_copy(k, dz):
        unit, row, rows = ITEMS[k]
        start, size = row_range(unit[1], half, half)
        return pltpu.make_async_remote_copy(
            src_ref=tok.at[pl.ds(2 * slot_of(unit), 2), pl.ds(row, rows), pl.ds(start, size)],
            dst_ref=rf.at[role(unit)[2], dz - 1, :, pl.ds(row, rows), pl.ds(start, size)],
            send_sem=fs.at[k],
            recv_sem=fr.at[k, dz - 1],
            device_id=near["z%d" % (4 - dz)],
            device_id_type=MESH,
        )

    def out_cols(lane, h, start):
        return pl.multiple_of((c + lane * (1 - 2 * c)) * chunk + h * half + start, 128)

    def y_copy(k, lane):
        unit, row, rows = ITEMS[k]
        start, size = row_range(unit[1], half, half)
        return pltpu.make_async_remote_copy(
            src_ref=tok.at[2 * slot_of(unit) + lane, pl.ds(row, rows), pl.ds(start, size)],
            dst_ref=out_ref.at[pl.ds(row, rows), pl.ds(out_cols(lane, ylo, start), size)],
            send_sem=ys.at[k, lane],
            recv_sem=yr.at[k, lane],
            device_id=near["yl"],
            device_id_type=MESH,
        )

    def part_item(k):
        unit, row, rows = ITEMS[k]
        slot = slot_of(unit)
        start, size = row_range(unit[1], half, half)
        if row == 0:
            go.shared(unit)

        @pl.loop(0, 2)
        def _(lane):
            by_head = (((1,), (1,)), ((), ()))
            total = lax.dot_general(
                mixed[0, row:row + rows],
                wo[lane, slot, 0, start:start + size, :],
                by_head,
                preferred_element_type=F32,
            )
            total += lax.dot_general(
                mixed[1, row:row + rows],
                wo[lane, slot, 1, start:start + size, :],
                by_head,
                preferred_element_type=F32,
            )
            tok[2 * slot + lane, row:row + rows, start:start + size] = total.astype(BF16)

        dz, _, _ = role(unit)
        for d in range(1, 4):

            @pl.when(dz == d)
            def _():
                z_copy(k, d).start()

    STEP = 64

    def collect(k):
        unit, row, rows = ITEMS[k]
        slot = slot_of(unit)
        start, size = row_range(unit[1], half, half)
        dz, _, ylos = role(unit)

        @pl.when(dz == 0)
        def _():
            for d in range(1, 4):
                z_copy(k, d).wait_recv()

            def summed(j):
                lane = j // (rows // STEP)
                at = pl.ds(pl.multiple_of(row + (j % (rows // STEP)) * STEP, STEP), STEP)
                total = tok[2 * slot + lane, at, start:start + size].astype(F32)
                for d in range(3):
                    total += rf[ylos, d, lane, at, start:start + size].astype(F32)
                return lane, at, total.astype(BF16)

            @pl.when(ylos == ylo)
            def _():
                @pl.loop(0, 2 * (rows // STEP))
                def _(j):
                    lane, at, total = summed(j)
                    out_ref[at, pl.ds(out_cols(lane, ylo, start), size)] = total

            @pl.when(ylos != ylo)
            def _():
                @pl.loop(0, 2 * (rows // STEP))
                def _(j):
                    lane, at, total = summed(j)
                    tok[2 * slot + lane, at, start:start + size] = total

                for lane in range(2):
                    y_copy(k, lane).start()

    for what, k in PLAN:
        if what == "mixed":
            swap_mixed(k).wait_recv()
        elif what == "event":
            go.event(k)
        elif what == "part":
            part_item(k)
        else:
            collect(k)

    gq.finish()
    go.finish()
    swap_o.wait_send()
    for b in range(2):
        swap_mixed(b).wait_send()
    for k in range(len(ITEMS)):
        dz, _, ylos = role(ITEMS[k][0])
        for d in range(1, 4):

            @pl.when(dz == d)
            def _():
                z_copy(k, d).wait_send()

        @pl.when((dz == 0) & (ylos != ylo))
        def _():
            for lane in range(2):
                y_copy(k, lane).wait_send()

        @pl.when((dz == 0) & (ylos == ylo))
        def _():
            for lane in range(2):
                y_copy(k, lane).wait_recv()


def layer(tokens, wq, wkv, wo, bias):
    count, model = tokens.shape
    rows, cols = wq.shape
    any_ = pl.BlockSpec(memory_space=pl.ANY)
    vmem = pl.BlockSpec(memory_space=pltpu.VMEM)
    dma = pltpu.SemaphoreType.DMA
    n = len(ITEMS)
    return pl.pallas_call(
        layer_kernel,
        name="layer",
        out_shape=(
            jax.ShapeDtypeStruct((count, cols), BF16),
            jax.ShapeDtypeStruct((count, 256), BF16),
        ),
        in_specs=[any_, any_, any_, any_, vmem],
        out_specs=(vmem, vmem),
        scratch_shapes=[
            pltpu.VMEM((16, count, 512), BF16),
            pltpu.VMEM((2, 8, rows, cols), BF16),
            pltpu.VMEM((2, 8, 2, rows // 2, cols), BF16),
            pltpu.VMEM((count, cols), F32),
            pltpu.VMEM((count, cols), BF16),
            pltpu.VMEM((2, count, cols), BF16),
            pltpu.VMEM((2, 3, 2, count, 256), BF16),
            pltpu.VMEM((2, 512, 256), BF16),
            dma((len(MOVES_Q),)), dma((len(MOVES_Q),)), dma((len(MOVES_O),)), dma((len(MOVES_O),)),
            dma((2,)), dma((2,)), dma((1,)), dma((1,)),
            dma((n,)), dma((n, 3)), dma((n, 2)), dma((n, 2)),
            dma((16,)), dma((2,)), dma((2,)),
        ],
        compiler_params=pltpu.CompilerParams(
            collective_id=0, has_side_effects=True, vmem_limit_bytes=63 * 2**20
        ),
    )(tokens, wq, wkv, wo, bias)


def segment_ids(lens, count):
    ends = jnp.cumsum(lens)
    position = jnp.arange(count, dtype=jnp.int32)
    return jnp.sum((position[:, None] >= ends[None, :]).astype(jnp.int32), axis=1)


def window_bias(lens, count):
    seg = segment_ids(lens, count)
    out = []
    for b in range(count // 128):
        first = max(b - 1, 0) * 128
        rows = jnp.arange(b * 128, b * 128 + 128, dtype=jnp.int32)
        cols = jnp.arange(first, first + 256, dtype=jnp.int32)
        ok = (seg[b * 128:b * 128 + 128, None] == seg[None, first:first + 256]) & (cols[None, :] <= rows[:, None])
        out.append(jnp.where(ok, 0.0, NEG).astype(F32))
    return jnp.stack(out)


def decode_attend(query, cache, fresh, stretch, cache_rows, stretch_rows):
    steps, rows = (query.shape[0], query.shape[1])
    heads = stretch.shape[2]
    width = stretch.shape[3] // 2
    group = query.shape[2] // (heads * width)
    span = cache.shape[2]
    most = stretch.shape[1]
    scale = width ** (-0.5)
    f32 = jnp.float32
    q_five = query.reshape(steps, rows, heads, group, width)
    ckeys = cache[0].reshape(rows, span, heads, width)
    cvals = cache[1].reshape(rows, span, heads, width)
    nkeys = stretch[..., :width]
    nvals = stretch[..., width:]
    fkeys = fresh[0].reshape(steps, rows, heads, width)
    fvals = fresh[1].reshape(steps, rows, heads, width)
    s_cache = jnp.einsum("trhgd,rchd->rhtgc", q_five, ckeys, preferred_element_type=f32) * scale
    s_new = jnp.einsum("trhgd,rnhd->rhtgn", q_five, nkeys, preferred_element_type=f32) * scale
    s_fresh = jnp.einsum("trhgd,urhd->rhtgu", q_five, fkeys, preferred_element_type=f32) * scale
    mask_cache = jnp.arange(span, dtype=jnp.int32)[None, :] < cache_rows[:, None]
    mask_new = jnp.arange(most, dtype=jnp.int32)[None, :] < stretch_rows[:, None]
    mask_fresh = jnp.arange(steps)[None, :] <= jnp.arange(steps)[:, None]
    s_cache = jnp.where(mask_cache[:, None, None, None, :], s_cache, NEG)
    s_new = jnp.where(mask_new[:, None, None, None, :], s_new, NEG)
    s_fresh = jnp.where(mask_fresh[None, None, :, None, :], s_fresh, NEG)
    top = jnp.maximum(
        jnp.maximum(jnp.max(s_cache, axis=-1), jnp.max(s_new, axis=-1)), jnp.max(s_fresh, axis=-1)
    )[..., None]
    e_cache = jnp.exp(s_cache - top)
    e_new = jnp.exp(s_new - top)
    e_fresh = jnp.exp(s_fresh - top)
    total = jnp.sum(e_cache, axis=-1) + jnp.sum(e_new, axis=-1) + jnp.sum(e_fresh, axis=-1)
    acc = jnp.einsum(
        "rhtgc,rchd->trhgd", e_cache.astype(jnp.bfloat16), cvals, preferred_element_type=f32
    )
    acc = acc + jnp.einsum(
        "rhtgn,rnhd->trhgd", e_new.astype(jnp.bfloat16), nvals, preferred_element_type=f32
    )
    acc = acc + jnp.einsum(
        "rhtgu,urhd->trhgd", e_fresh.astype(jnp.bfloat16), fvals, preferred_element_type=f32
    )
    mixed = acc / jnp.transpose(total, (2, 0, 1, 3))[..., None]
    return mixed.astype(jnp.bfloat16).reshape(steps, rows, heads * group * width)


def local(
    tokens, w_query, w_keyval, output_weight, cache, fresh, decode_query, cache_len, new_len, route
):
    count, model = tokens.shape
    heads = w_keyval.shape[1]
    width = w_keyval.shape[2] // 2
    groups, slots = (route.shape[0], route.shape[1])
    my_group = lax.axis_index("req")
    my_lens = lax.dynamic_index_in_dim(new_len, my_group, 0, keepdims=False)
    prefill_out, keyval = layer(
        tokens,
        w_query.reshape(w_query.shape[0], -1),
        w_keyval.reshape(model, -1),
        output_weight.reshape(output_weight.shape[0], -1),
        window_bias(my_lens, count),
    )
    offsets = jnp.cumsum(my_lens) - my_lens
    my_route = lax.dynamic_index_in_dim(route, my_group, 0, keepdims=False)
    ranks = jnp.arange(groups, dtype=jnp.int32)
    hit_send = (my_route[None, :] == ranks[:, None]).astype(jnp.int32)
    start = jnp.sum(hit_send * offsets[None, :], axis=1)
    most = 2 * count // slots
    cols = keyval.shape[1]
    padded = jnp.concatenate([keyval, jnp.zeros((most, cols), jnp.bfloat16)], axis=0)
    index = start[:, None] + jnp.arange(most, dtype=jnp.int32)[None, :]
    outgoing = padded[index]
    incoming = lax.all_to_all(outgoing, "req", split_axis=0, concat_axis=0, tiled=True)
    hit_recv = (route == my_group).astype(jnp.int32)
    stretch_rows = jnp.sum(hit_recv * new_len, axis=1)
    stretch = incoming.reshape(groups, most, heads, 2 * width)
    decode_out = decode_attend(
        decode_query, cache, fresh, stretch, cache_len.reshape(-1), stretch_rows
    )
    return (prefill_out, decode_out)


def solution(mesh):
    placed = (
        P("req", None),
        P("req", "tp", None),
        P(None, "tp", None),
        P("req", "tp", None),
        P(None, "req", None, "tp"),
        P(None, None, "req", "tp"),
        P(None, "req", "tp"),
        P("req", None),
        P(),
        P(),
    )
    return jax.shard_map(
        local,
        mesh=mesh,
        in_specs=placed,
        out_specs=(P("req", "tp"), P(None, "req", "tp")),
        check_vma=False,
    )
```

time: 300 us -> 218 us (0.73)
  the two profiles are of different devices: /device:TPU:24 before, /device:TPU:1 now
where the time goes in v2:
time: 218 us
  Pallas kernels  172 us (79%)
  starting transfers between devices  17.8 us (8%)
  local copies, waits for them, and re-layouts  8.59 us (4%)
  matrix products  8.45 us (4%)
  waiting for transfers between devices  6.57 us (3%)
  other arithmetic  3.66 us (2%)
    pallas_call x1, Pallas kernels, layer(): pl.pallas_call(layer_kernel, name='layer', out_shape=(jax.ShapeDtypeStruc...  172 us
    all_to_all x1, starting transfers between devices, local(): lax.all_to_all(outgoing, 'req', split_axis=0, concat_axis=0, tiled=True)  17.8 us
    all_to_all x1, waiting for transfers between devices, local(): lax.all_to_all(outgoing, 'req', split_axis=0, concat_axis=0, tiled=True)  6.57 us
    gather x1, local copies, waits for them, and re-layouts, local(): outgoing = padded[index]  4.98 us
  transfers between devices with their start and end apart: 1, of which 1 were waited for; matrix products, arithmetic and copies ran while one was open for 2% of the time, Pallas kernels for 0%

profile of v2, /device:TPU:1, one launch (start us, length us, event | category | flops | bytes accessed | tf_op | source)
XLA Modules:
  0.0 217.8 jit_solution(17671490823987932627)
XLA Ops:
  0.6 0.7 fusion.40
  1.5 0.1 reduce.12
  1.7 0.7 fusion.39
  2.4 0.1 select_reduce_fusion
  2.7 0.1 and_select_fusion.1
  2.8 0.2 fusion.29
  3.0 0.8 pad_maximum_fusion.bias_ref
  3.8 171.9 %layer.1 = (bf16[512,1024]{1,0:T(8,128)(2,1)}, bf16[512,256]{1,0:T(8,128)(2,1)}) custom-call(bf16[512,8192]{1,0:T(8,128)(2,1)} %tok_hbm.1, bf16[512,1024]{1,0:T(8,128)(2,1)} %bitcast.113, bf16[8192,256]{1,0:T(8,128)(2,1)} %bitcast.112, bf16[512,1024]{1,0:T(8,128)(2,1)} %bitcast.114, f32[4,128,256]{2,1,0:T(8,128)} %pad_maximum_fusion.bias_ref), custom_call_target="tpu_custom_call" | custom-call | tf_op jit(solution)/shard_map/layer/pallas_call | solution.py:438
  175.7 1.0 concatenate.3
  176.7 5.0 %gather_fusion = bf16[1024,256]{1,0:T(8,128)(2,1)} fusion(bf16[576,256]{1,0:T(8,128)(2,1)S(1)} %concatenate.3, s32[1024]{0:T(1024)S(1)} %broadcast_clamp_fusion), kind=kCustom, calls=%fused_computation | custom fusion | bytes 1052672 | tf_op jit(solution)/shard_map/gather | solution.py:555
  181.7 17.8 %all-to-all-start = ((bf16[16,64,256]{2,1,0:T(8,128)(2,1)}), bf16[16,64,256]{2,1,0:T(8,128)(2,1)S(1)}, u32[]{:S(2)}, u32[]{:S(2)}) async-start(bf16[16,64,256]{2,1,0:T(8,128)(2,1)} %bitcast.10), calls=%async_computation | async-start | bytes 1048576 | tf_op jit(solution)/shard_map/all_to_all | solution.py:556
  199.5 0.1 select_reduce_fusion.1
  199.8 0.7 fusion.46
  200.6 3.7 %fusion.6 = (f32[16,4,8]{2,1,0:T(4,128)S(1)}, f32[16,4,8,1024]{3,2,1,0:T(8,128)S(1)}) fusion(pred[16,1024]{1,0:T(8,128)(4,1)S(1)} %iota_compare_fusion.2, bf16[2,16,1024,128]{3,2,1,0:T(8,128)(2,1)} %param.14, bf16[4,16,8,128]{3,2,1,0:T(8,128)(2,1)S(1)} %bitcast.122), kind=kOutput, calls=%fused_computation.9 | convolution fusion | flops 135790080 | bytes 6440960 | tf_op jit(solution)/shard_map/trhgd,rchd->rhtgc/dot_general | solution.py:501
  204.3 6.6 %all-to-all-done = bf16[16,64,256]{2,1,0:T(8,128)(2,1)S(1)} async-done(((bf16[16,64,256]{2,1,0:T(8,128)(2,1)}), bf16[16,64,256]{2,1,0:T(8,128)(2,1)S(1)}, u32[]{:S(2)}, u32[]{:S(2)}) %all-to-all-start) | async-done | bytes 524320 | tf_op jit(solution)/shard_map/all_to_all | solution.py:556
  210.9 0.3 fusion.47
  211.2 0.6 fusion.7
  211.9 3.2 %fusion.9 = f32[16,128,4,8]{1,3,2,0:T(8,128)S(1)} fusion(bf16[2,16,1024,128]{3,2,1,0:T(8,128)(2,1)} %param.14, f32[16,4,8,1024]{3,2,1,0:T(8,128)S(1)} %get-tuple-element.26, f32[16,4,8]{2,1,0:T(4,128)S(1)} %bitcast.116, pred[16,1024]{1,0:T(8,128)(4,1)S(1)} %iota_compare_fusion.2), kind=kOutput, calls=%fused_computation.12 | convolution fusion | flops 136314880 | bytes 6572032 | tf_op jit(solution)/shard_map/rhtgc,rchd->trhgd/dot_general | solution.py:517
  215.1 0.3 fusion.24
  215.4 0.1 fusion.32
  215.5 0.2 convolution_bitcast_fusion
  215.8 0.3 fusion.18
  216.1 0.7 copy.32
  216.8 1.0 copy.61
  (33 shorter events, 0.7 us)
Async XLA Ops:
  176.7 22.8 %copy-start.3 = (s32[16,16]{1,0:T(8,128)S(1)}, s32[16,16]{1,0:T(8,128)}, u32[]{:S(2)}) copy-start(s32[16,16]{1,0:T(8,128)} %param.18) | copy-start | bytes 3076
  176.7 22.8 %copy-start.4 = (s32[16,16]{1,0:T(8,128)S(1)}, s32[16,16]{1,0:T(8,128)}, u32[]{:S(2)}) copy-start(s32[16,16]{1,0:T(8,128)} %param.19) | copy-start | bytes 3076
  176.7 22.9 %copy-start.1 = (bf16[4,16,1024]{2,1,0:T(8,128)(2,1)S(1)}, bf16[4,16,1024]{2,1,0:T(8,128)(2,1)}, u32[]{:S(2)}) copy-start(bf16[4,16,1024]{2,1,0:T(8,128)(2,1)} %param.16) | copy-start | bytes 393220
  176.7 22.9 %copy-start.5 = (s32[1,16]{1,0:T(1,128)S(1)}, s32[1,16]{1,0:T(1,128)}, u32[]{:S(2)}) copy-start(s32[1,16]{1,0:T(1,128)} %param.17) | copy-start | bytes 196
  176.7 23.0 %copy-start.2 = (bf16[2,4,16,128]{3,2,1,0:T(8,128)(2,1)S(1)}, bf16[2,4,16,128]{3,2,1,0:T(8,128)(2,1)}, u32[]{:S(2)}) copy-start(bf16[2,4,16,128]{3,2,1,0:T(8,128)(2,1)} %param.15) | copy-start | bytes 98308
  181.7 29.2 %all-to-all-start = ((bf16[16,64,256]{2,1,0:T(8,128)(2,1)}), bf16[16,64,256]{2,1,0:T(8,128)(2,1)S(1)}, u32[]{:S(2)}, u32[]{:S(2)}) async-start(bf16[16,64,256]{2,1,0:T(8,128)(2,1)} %bitcast.10), calls=%async_computation | async-start | bytes 1048576 | tf_op jit(solution)/shard_map/all_to_all | solution.py:556
  215.1 1.7 copy-start

commit v3 on v2

--- a/solution.py
+++ b/solution.py
@@ -75,8 +75,10 @@
 PLAN = (
     [("mixed", 0), ("part", 0), ("part", 1), ("event", 1), ("part", 2), ("part", 3), ("mixed", 1)]
     + [("part", i) for i in range(4, 8)]
+    + [("decode", r) for r in range(9, 13)]
     + [("event", 2), ("collect", 0), ("collect", 1), ("part", 8), ("part", 9)]
     + [("collect", i) for i in range(2, 8)]
+    + [("decode", r) for r in range(13, 16)]
     + [("event", 3), ("event", 4), ("part", 10), ("part", 11), ("collect", 8), ("collect", 9)]
     + [("event", 5), ("part", 12), ("part", 13), ("event", 6), ("part", 14), ("part", 15)]
     + [("collect", i) for i in range(10, 16)]
@@ -158,10 +160,10 @@
 
 
 def layer_kernel(
-    tok_hbm, wq_hbm, wkv_hbm, wo_hbm, bias_ref,
-    out_ref, kv_ref,
-    tok, wq, wo, acc, query, mixed, rf, wkv,
-    qs, qr, os_, or_, ms, mr, ps, pr, fs, fr, ys, yr, tsem, ksem, lsem,
+    tok_hbm, wq_hbm, wkv_hbm, wo_hbm, bias_ref, cache_hbm, fresh_ref, dq_ref, sel_ref, lens_ref,
+    out_ref, dec_ref,
+    tok, wq, wo, acc, query, mixed, rf, wkv, kv_ref, outgoing, stretch, cbuf,
+    qs, qr, os_, or_, ms, mr, ps, pr, fs, fr, ys, yr, tsem, ksem, lsem, hs, hr, csem,
 ):
     z, ylo, yhi, x, c = where_am_i()
     near = neighbours()
@@ -176,10 +178,15 @@
     )
     own_q.start()
 
+    tp = z * 2 + ylo
+    req = yhi * 8 + x * 2 + c
+    groups = stretch.shape[0]
     barrier = pltpu.get_barrier_semaphore()
-    for way in near:
+    for way in ("z1", "z2", "z3", "yl"):
         pl.semaphore_signal(barrier, inc=1, device_id=near[way], device_id_type=MESH)
-    pl.semaphore_wait(barrier, len(near))
+    for i in range(1, groups):
+        pl.semaphore_signal(barrier, inc=1, device_id=(tp, (req + i) % groups), device_id_type=MESH)
+    pl.semaphore_wait(barrier, 4 + groups - 1)
 
     gq = Gather(lambda lane, slot, rows: wq.at[lane, slot, rows], MOVES_Q, EVENTS_Q, chunk, CUT_Q, qs, qr, near)
     go = Gather(lambda lane, slot, rows: wo.at[lane, slot, :, rows], MOVES_O, EVENTS_O, half, half, os_, or_, near)
@@ -220,6 +227,61 @@
 
     kv_ref[...] = acc[:, 0:256].astype(BF16)
     acc[...] = jnp.zeros_like(acc)
+
+    most = stretch.shape[1]
+    outgoing[...] = (
+        jnp.dot(sel_ref[...], kv_ref[...], preferred_element_type=F32).astype(BF16).reshape(groups, most, 256)
+    )
+
+    def handoff(i):
+        to = (req + i) % groups
+        return pltpu.make_async_remote_copy(
+            src_ref=outgoing.at[to],
+            dst_ref=stretch.at[req],
+            send_sem=hs.at[i],
+            recv_sem=hr.at[i],
+            device_id=(tp, to),
+            device_id_type=MESH,
+        )
+
+    for i in range(1, groups):
+        handoff(i).start()
+    stretch[req] = outgoing[req]
+
+    def cache_copy(r):
+        return pltpu.make_async_copy(cache_hbm.at[:, r], cbuf.at[r % 2], csem.at[r % 2])
+
+    cache_copy(0).start()
+    cache_copy(1).start()
+
+    def decode(r):
+        if r == 0:
+            for i in range(1, groups):
+                handoff(i).wait_recv()
+        cache_copy(r).wait()
+        slot = r % 2
+        span = cbuf.shape[2]
+        by_head = (((1,), (1,)), ((), ()))
+        q = dq_ref[r]
+        s = lax.dot_general(q, cbuf[slot, 0], by_head, preferred_element_type=F32) * scale
+        col = lax.broadcasted_iota(jnp.int32, (32, span), 1)
+        s = jnp.where(col < lens_ref[0, r], s, NEG)
+        keys = jnp.concatenate([stretch[r, :, 0:128], fresh_ref[r, 0]], axis=0)
+        values = jnp.concatenate([stretch[r, :, 128:256], fresh_ref[r, 1]], axis=0)
+        t = lax.dot_general(q, keys, by_head, preferred_element_type=F32) * scale
+        col = lax.broadcasted_iota(jnp.int32, (32, 2 * most), 1)
+        step = lax.broadcasted_iota(jnp.int32, (32, 2 * most), 0) >> 3
+        ok = (col < lens_ref[1, r]) | ((col >= most) & (col - most <= step))
+        t = jnp.where(ok, t, NEG)
+        top = jnp.maximum(jnp.max(s, axis=1, keepdims=True), jnp.max(t, axis=1, keepdims=True))
+        e = jnp.exp(s - top)
+        f = jnp.exp(t - top)
+        total = jnp.sum(e, axis=1, keepdims=True) + jnp.sum(f, axis=1, keepdims=True)
+        got = jnp.dot(e.astype(BF16), cbuf[slot, 1], preferred_element_type=F32)
+        got += jnp.dot(f.astype(BF16), values, preferred_element_type=F32)
+        dec_ref[r] = (got / total).astype(BF16)
+        if r + 2 < groups:
+            cache_copy(r + 2).start()
 
     def place(unit):
         (dx, dy), part = unit
@@ -259,6 +321,8 @@
         for unit in waiting:
             query_unit(unit)
         waiting = EVENTS_Q[k][2]
+        if k >= 1:
+            decode(k - 1)
     for unit in waiting:
         query_unit(unit)
     query[...] = acc[...].astype(BF16)
@@ -401,12 +465,16 @@
             go.event(k)
         elif what == "part":
             part_item(k)
+        elif what == "decode":
+            decode(k)
         else:
             collect(k)
 
     gq.finish()
     go.finish()
     swap_o.wait_send()
+    for i in range(1, groups):
+        handoff(i).wait_send()
     for b in range(2):
         swap_mixed(b).wait_send()
     for k in range(len(ITEMS)):
@@ -428,8 +496,9 @@
                 y_copy(k, lane).wait_recv()
 
 
-def layer(tokens, wq, wkv, wo, bias):
+def layer(tokens, wq, wkv, wo, bias, cache, fresh, decode_query, sel, lens):
     count, model = tokens.shape
+    requests, most, span = (fresh.shape[0], fresh.shape[2], cache.shape[2])
     rows, cols = wq.shape
     any_ = pl.BlockSpec(memory_space=pl.ANY)
     vmem = pl.BlockSpec(memory_space=pltpu.VMEM)
@@ -440,9 +509,9 @@
         name="layer",
         out_shape=(
             jax.ShapeDtypeStruct((count, cols), BF16),
-            jax.ShapeDtypeStruct((count, 256), BF16),
+            jax.ShapeDtypeStruct(decode_query.shape, BF16),
         ),
-        in_specs=[any_, any_, any_, any_, vmem],
+        in_specs=[any_, any_, any_, any_, vmem, any_, vmem, vmem, vmem, pl.BlockSpec(memory_space=pltpu.SMEM)],
         out_specs=(vmem, vmem),
         scratch_shapes=[
             pltpu.VMEM((16, count, 512), BF16),
@@ -453,15 +522,19 @@
             pltpu.VMEM((2, count, cols), BF16),
             pltpu.VMEM((2, 3, 2, count, 256), BF16),
             pltpu.VMEM((2, 512, 256), BF16),
+            pltpu.VMEM((count, 256), BF16),
+            pltpu.VMEM((requests, most, 256), BF16),
+            pltpu.VMEM((requests, most, 256), BF16),
+            pltpu.VMEM((2, 2, span, 128), BF16),
             dma((len(MOVES_Q),)), dma((len(MOVES_Q),)), dma((len(MOVES_O),)), dma((len(MOVES_O),)),
             dma((2,)), dma((2,)), dma((1,)), dma((1,)),
             dma((n,)), dma((n, 3)), dma((n, 2)), dma((n, 2)),
-            dma((16,)), dma((2,)), dma((2,)),
+            dma((16,)), dma((2,)), dma((2,)), dma((requests,)), dma((requests,)), dma((2,)),
         ],
         compiler_params=pltpu.CompilerParams(
             collective_id=0, has_side_effects=True, vmem_limit_bytes=63 * 2**20
         ),
-    )(tokens, wq, wkv, wo, bias)
+    )(tokens, wq, wkv, wo, bias, cache, fresh, decode_query, sel, lens)
 
 
 def segment_ids(lens, count):
@@ -482,84 +555,42 @@
     return jnp.stack(out)
 
 
-def decode_attend(query, cache, fresh, stretch, cache_rows, stretch_rows):
-    steps, rows = (query.shape[0], query.shape[1])
-    heads = stretch.shape[2]
-    width = stretch.shape[3] // 2
-    group = query.shape[2] // (heads * width)
-    span = cache.shape[2]
-    most = stretch.shape[1]
-    scale = width ** (-0.5)
-    f32 = jnp.float32
-    q_five = query.reshape(steps, rows, heads, group, width)
-    ckeys = cache[0].reshape(rows, span, heads, width)
-    cvals = cache[1].reshape(rows, span, heads, width)
-    nkeys = stretch[..., :width]
-    nvals = stretch[..., width:]
-    fkeys = fresh[0].reshape(steps, rows, heads, width)
-    fvals = fresh[1].reshape(steps, rows, heads, width)
-    s_cache = jnp.einsum("trhgd,rchd->rhtgc", q_five, ckeys, preferred_element_type=f32) * scale
-    s_new = jnp.einsum("trhgd,rnhd->rhtgn", q_five, nkeys, preferred_element_type=f32) * scale
-    s_fresh = jnp.einsum("trhgd,urhd->rhtgu", q_five, fkeys, preferred_element_type=f32) * scale
-    mask_cache = jnp.arange(span, dtype=jnp.int32)[None, :] < cache_rows[:, None]
-    mask_new = jnp.arange(most, dtype=jnp.int32)[None, :] < stretch_rows[:, None]
-    mask_fresh = jnp.arange(steps)[None, :] <= jnp.arange(steps)[:, None]
-    s_cache = jnp.where(mask_cache[:, None, None, None, :], s_cache, NEG)
-    s_new = jnp.where(mask_new[:, None, None, None, :], s_new, NEG)
-    s_fresh = jnp.where(mask_fresh[None, None, :, None, :], s_fresh, NEG)
-    top = jnp.maximum(
-        jnp.maximum(jnp.max(s_cache, axis=-1), jnp.max(s_new, axis=-1)), jnp.max(s_fresh, axis=-1)
-    )[..., None]
-    e_cache = jnp.exp(s_cache - top)
-    e_new = jnp.exp(s_new - top)
-    e_fresh = jnp.exp(s_fresh - top)
-    total = jnp.sum(e_cache, axis=-1) + jnp.sum(e_new, axis=-1) + jnp.sum(e_fresh, axis=-1)
-    acc = jnp.einsum(
-        "rhtgc,rchd->trhgd", e_cache.astype(jnp.bfloat16), cvals, preferred_element_type=f32
-    )
-    acc = acc + jnp.einsum(
-        "rhtgn,rnhd->trhgd", e_new.astype(jnp.bfloat16), nvals, preferred_element_type=f32
-    )
-    acc = acc + jnp.einsum(
-        "rhtgu,urhd->trhgd", e_fresh.astype(jnp.bfloat16), fvals, preferred_element_type=f32
-    )
-    mixed = acc / jnp.transpose(total, (2, 0, 1, 3))[..., None]
-    return mixed.astype(jnp.bfloat16).reshape(steps, rows, heads * group * width)
-
-
 def local(
     tokens, w_query, w_keyval, output_weight, cache, fresh, decode_query, cache_len, new_len, route
 ):
     count, model = tokens.shape
-    heads = w_keyval.shape[1]
+    groups, slots = (route.shape[0], route.shape[1])
+    steps, rows, qcols = decode_query.shape
     width = w_keyval.shape[2] // 2
-    groups, slots = (route.shape[0], route.shape[1])
+    heads = qcols // width
+    most = 2 * count // slots
     my_group = lax.axis_index("req")
     my_lens = lax.dynamic_index_in_dim(new_len, my_group, 0, keepdims=False)
-    prefill_out, keyval = layer(
+    offsets = jnp.cumsum(my_lens) - my_lens
+    my_route = lax.dynamic_index_in_dim(route, my_group, 0, keepdims=False)
+    ranks = jnp.arange(groups, dtype=jnp.int32)
+    hit_send = (my_route[None, :] == ranks[:, None]).astype(jnp.int32)
+    start = jnp.sum(hit_send * offsets[None, :], axis=1)
+    index = (start[:, None] + jnp.arange(most, dtype=jnp.int32)[None, :]).reshape(-1)
+    sel = (index[:, None] == jnp.arange(count, dtype=jnp.int32)[None, :]).astype(jnp.bfloat16)
+    hit_recv = (route == my_group).astype(jnp.int32)
+    stretch_rows = jnp.sum(hit_recv * new_len, axis=1)
+    lens = jnp.stack([cache_len.reshape(-1), stretch_rows])
+    extra = jnp.pad(jnp.transpose(fresh, (2, 0, 1, 3)), ((0, 0), (0, 0), (0, most - steps), (0, 0)))
+    dq = decode_query.reshape(steps, rows, heads, width).transpose(1, 0, 2, 3).reshape(rows, steps * heads, width)
+    prefill_out, decoded = layer(
         tokens,
         w_query.reshape(w_query.shape[0], -1),
         w_keyval.reshape(model, -1),
         output_weight.reshape(output_weight.shape[0], -1),
         window_bias(my_lens, count),
+        cache,
+        extra,
+        dq,
+        sel,
+        lens,
     )
-    offsets = jnp.cumsum(my_lens) - my_lens
-    my_route = lax.dynamic_index_in_dim(route, my_group, 0, keepdims=False)
-    ranks = jnp.arange(groups, dtype=jnp.int32)
-    hit_send = (my_route[None, :] == ranks[:, None]).astype(jnp.int32)
-    start = jnp.sum(hit_send * offsets[None, :], axis=1)
-    most = 2 * count // slots
-    cols = keyval.shape[1]
-    padded = jnp.concatenate([keyval, jnp.zeros((most, cols), jnp.bfloat16)], axis=0)
-    index = start[:, None] + jnp.arange(most, dtype=jnp.int32)[None, :]
-    outgoing = padded[index]
-    incoming = lax.all_to_all(outgoing, "req", split_axis=0, concat_axis=0, tiled=True)
-    hit_recv = (route == my_group).astype(jnp.int32)
-    stretch_rows = jnp.sum(hit_recv * new_len, axis=1)
-    stretch = incoming.reshape(groups, most, heads, 2 * width)
-    decode_out = decode_attend(
-        decode_query, cache, fresh, stretch, cache_len.reshape(-1), stretch_rows
-    )
+    decode_out = decoded.reshape(rows, steps, heads, width).transpose(1, 0, 2, 3).reshape(steps, rows, qcols)
     return (prefill_out, decode_out)
 
 

time: 218 us -> 206 us (0.945)
  the two profiles are of different devices: /device:TPU:1 before, /device:TPU:48 now
where the time goes in v3:
time: 206 us; the launch traced here: 205 us
  Pallas kernels  191 us (93%)
  local copies, waits for them, and re-layouts  8.07 us (4%)
  other arithmetic  5.56 us (3%)
    pallas_call x1, Pallas kernels, layer(): pl.pallas_call(layer_kernel, name='layer', out_shape=(jax.ShapeDtypeStruc...  191 us

profile of v3, /device:TPU:48, one launch (start us, length us, event | category | flops | bytes accessed | tf_op | source)
XLA Modules:
  0.0 205.1 jit_solution(3236280598663487465)
XLA Ops:
  0.6 0.8 select_reduce_fusion
  1.5 1.3 pad_add_fusion.lens_ref
  2.7 0.7 fusion.6
  3.4 0.1 copy.20
  3.6 0.1 reduce
  3.7 0.7 fusion.5
  4.4 0.1 select_reduce_fusion.1
  4.5 0.1 convert_reduce_fusion
  4.6 0.1 iota_add_fusion
  4.7 0.1 add.91
  4.8 0.8 copy.28
  5.5 0.1 and_select_fusion.1
  5.6 0.9 copy.25
  6.6 0.7 copy_bitcast_fusion.dq_ref
  7.2 0.1 fusion.2
  7.4 0.9 pad_maximum_fusion.bias_ref
  8.3 0.9 pad.4.fresh_ref
  9.2 1.2 fusion.sel_ref
  10.4 190.8 %layer.1 = (bf16[512,1024]{1,0:T(8,128)(2,1)}, bf16[16,32,128]{2,1,0:T(8,128)(2,1)}) custom-call(bf16[512,8192]{1,0:T(8,128)(2,1)} %tok_hbm.1, bf16[512,1024]{1,0:T(8,128)(2,1)} %bitcast.37, bf16[8192,256]{1,0:T(8,128)(2,1)} %bitcast.36, bf16[512,1024]{1,0:T(8,128)(2,1)} %bitcast.38, f32[4,128,256]{2,1,0:T(8,128)} %pad_maximum_fusion.bias_ref, ...), custom_call_target="tpu_custom_call" | custom-call | tf_op jit(solution)/shard_map/layer/pallas_call | solution.py:507
  201.2 0.9 reshape.404
  202.1 0.7 copy.24
  202.8 2.3 %copy.30 = bf16[512,1024]{1,0:T(8,128)(2,1)} copy(bf16[512,1024]{1,0:T(8,128)(2,1)} %get-tuple-element.20) | data formatting | bytes 2097152
  (8 shorter events, 0.1 us)

commit v4 on v3

v4 whole, which is shorter than its diff:
```python
import functools

import jax
import jax.numpy as jnp
from jax import lax
from jax.experimental import pallas as pl
from jax.experimental.pallas import tpu as pltpu
from jax.sharding import PartitionSpec as P

NEG = -1e30
MESH = pl.DeviceIdType.MESH
F32 = jnp.float32
BF16 = jnp.bfloat16

CUT_Q = 384
CUT_O = 128
START_O = 3

MOVES = {
    "yA": ((0, 0), "A", (0, 1), "y"),
    "xpA": ((0, 0), "A", (3, 0), "xp"),
    "xmA": ((0, 0), "A", (1, 0), "xm"),
    "xpB": ((0, 0), "B", (3, 0), "xp"),
    "xmB": ((0, 0), "B", (1, 0), "xm"),
    "xpC": ((0, 1), "A", (3, 1), "xp"),
    "xmC": ((0, 1), "A", (1, 1), "xm"),
    "fpA": ((3, 0), "A0", (2, 0), "xp"),
    "fmA": ((1, 0), "A1", (2, 0), "xm"),
    "fpC": ((3, 1), "A0", (2, 1), "xp"),
    "fmC": ((1, 1), "A1", (2, 1), "xm"),
    "fpB": ((3, 0), "B0", (2, 0), "xp"),
    "fmB": ((1, 0), "B1", (2, 0), "xm"),
    "yB0": ((0, 0), "B", (0, 1), "y"),
    "yBm": ((3, 0), "B", (3, 1), "y"),
    "yBp": ((1, 0), "B", (1, 1), "y"),
    "yB2p": ((2, 0), "B0", (2, 1), "y"),
    "yB2m": ((2, 0), "B1", (2, 1), "y"),
}
FIRST_A = ["yA", "xpA", "xmA", "s00A"]
FIRST_B = ["xpB", "xmB", "yB0", "s00B"]
EVENTS = [
    (["yA"], ["xpC", "xmC", "s01A"], [((0, 1), "A")]),
    (["xpA", "xmA"], ["fpA", "fmA", "s30A", "s10A"], [((3, 0), "A"), ((1, 0), "A")]),
    (["xpB", "xmB"], ["fpB", "fmB", "yBm", "yBp", "s30B", "s10B"], [((3, 0), "B"), ((1, 0), "B")]),
    (["xpC", "xmC"], ["fpC", "fmC", "s31A", "s11A"], [((3, 1), "A"), ((1, 1), "A")]),
    (["fpA", "fmA"], ["s20A"], [((2, 0), "A")]),
    (["fpB", "fmB"], ["yB2p", "yB2m", "s20B"], [((2, 0), "B")]),
    (["yB0"], ["s01B"], [((0, 1), "B")]),
    (["yBm", "yBp"], ["s31B", "s11B"], [((3, 1), "B"), ((1, 1), "B")]),
    (["fpC", "fmC"], ["s21A"], [((2, 1), "A")]),
    (["yB2p", "yB2m"], ["s21B"], [((2, 1), "B")]),
]
UNITS = [((0, 0), "A"), ((0, 0), "B")] + [u for e in EVENTS for u in e[2]]
MOVES_ALL = {**MOVES, **{"s%d%d%s" % (slot + (part,)): (slot, part, slot, "sib") for slot, part in UNITS}}
EVENTS_O = [EVENTS[k] for k in (2, 0, 1, 5, 3, 4, 6, 7, 8, 9)]
START_1 = ["xpB", "xmB", "yA", "s00B"]
START_2 = ["xpA", "xmA", "yB0", "s00A"]
EARLY = [((0, 0), "AB"), ((0, 1), "A"), ((3, 0), "AB"), ((1, 0), "AB")]
LATE = [((3, 1), "A"), ((1, 1), "A"), ((2, 0), "AB"), ((0, 1), "B"), ((3, 1), "B"), ((1, 1), "B"), ((2, 1), "A"), ((2, 1), "B")]
ITEMS = [e + (r, 256) for r in (0, 256) for e in EARLY] + [e + (0, 512) for e in LATE]


def span(what, first, last):
    return [(what, k) for k in range(first, last)]


PLAN = (
    [("event", 2), ("mixed", 0)] + span("part", 0, 2) + [("event", 3)] + span("part", 2, 4) + [("mixed", 1)] + span("part", 4, 8)
    + [("event", 4)] + span("decode", 9, 13) + span("part", 8, 10) + [("event", 5), ("part", 10), ("event", 6), ("part", 11)]
    + span("decode", 13, 16) + span("collect", 0, 4) + [("event", 7)] + span("part", 12, 14) + span("collect", 4, 8)
    + [("event", 8), ("part", 14), ("event", 9), ("part", 15)] + span("collect", 8, 16)
)


def where_am_i():
    tp = lax.axis_index("tp")
    req = lax.axis_index("req")
    return tp // 2, tp % 2, req // 8, (req // 2) % 4, req % 2


def neighbours():
    z, ylo, yhi, x, c = where_am_i()
    tp = z * 2 + ylo
    req = yhi * 8 + x * 2 + c
    return {
        "xp": (tp, yhi * 8 + ((x + 1) % 4) * 2 + c),
        "xm": (tp, yhi * 8 + ((x + 3) % 4) * 2 + c),
        "y": (tp, (1 - yhi) * 8 + x * 2 + c),
        "y3": (z * 2 + (1 - ylo), (1 - yhi) * 8 + x * 2 + c),
        "sib": (tp, yhi * 8 + x * 2 + (1 - c)),
        "z1": (((z + 1) % 4) * 2 + ylo, req),
        "z2": (((z + 2) % 4) * 2 + ylo, req),
        "z3": (((z + 3) % 4) * 2 + ylo, req),
        "yl": (z * 2 + (1 - ylo), req),
    }


def row_range(part, cut, rows):
    rest = rows - cut
    return {
        "A": (0, cut),
        "A0": (0, cut // 2),
        "A1": (cut // 2, cut // 2),
        "B": (cut, rest),
        "B0": (cut, rest // 2),
        "B1": (cut + rest // 2, rest // 2),
        "AB": (0, rows),
    }[part]


class Gather:
    def __init__(self, view, events, rows, cut, send, recv, near):
        self.view, self.moves, self.events = view, MOVES_ALL, events
        self.rows, self.cut, self.send, self.recv, self.near = rows, cut, send, recv, near
        self.index = {name: i for i, name in enumerate(MOVES_ALL)}

    def copy(self, name):
        src, part, dst, way = self.moves[name]
        start, size = row_range(part, self.cut, self.rows)
        lane = 1 if way == "sib" else 0
        i = self.index[name]
        return pltpu.make_async_remote_copy(
            src_ref=self.view(0, src[1] * 4 + src[0], pl.ds(start, size)),
            dst_ref=self.view(lane, dst[1] * 4 + dst[0], pl.ds(start, size)),
            send_sem=self.send.at[i],
            recv_sem=self.recv.at[i],
            device_id=self.near[way],
            device_id_type=MESH,
        )

    def start(self, names):
        for name in names:
            self.copy(name).start()

    def event(self, k):
        waits, starts, _ = self.events[k]
        for name in waits:
            self.copy(name).wait_recv()
        self.start(starts)

    def shared(self, slot, parts):
        for part in parts:
            self.copy("s%d%d%s" % (slot + (part,))).wait_recv()

    def finish(self):
        for name in self.moves:
            self.copy(name).wait_send()


def layer_kernel(
    tok_hbm, wq_hbm, wkv_hbm, wo_hbm, cache_hbm, fresh_ref, dq_ref, held_ref, new_ref, route_ref,
    out_ref, dec_ref,
    tok, wq, wo, acc, query, mixed, rf, wkv, kvs, outgoing, stretch, cbuf,
    qs, qr, os_, or_, ms, mr, ps, pr, fs, fr, ys, yr, tsem, ksem, lsem, hs, hr, csem,
):
    z, ylo, yhi, x, c = where_am_i()
    near = neighbours()
    count = tok.shape[1]
    chunk = tok.shape[2]
    half = chunk // 2
    scale = 128 ** -0.5

    e = (ylo + yhi) % 2
    own_half = pl.ds(pl.multiple_of(e * half, half), half)
    other_half = pl.ds(pl.multiple_of((1 - e) * half, half), half)
    own_q = pltpu.make_async_copy(wq_hbm, wq.at[0, 0], lsem.at[0])
    own_o = pltpu.make_async_copy(wo_hbm.at[own_half], wo.at[0, 0, ylo], lsem.at[1])
    own_q.start()
    own_o.start()

    tp = z * 2 + ylo
    req = yhi * 8 + x * 2 + c
    groups = stretch.shape[0]
    barrier = pltpu.get_barrier_semaphore()
    for way in ("z1", "z2", "z3", "yl", "y3"):
        pl.semaphore_signal(barrier, inc=1, device_id=near[way], device_id_type=MESH)
    for i in range(1, groups):
        pl.semaphore_signal(barrier, inc=1, device_id=(tp, (req + i) % groups), device_id_type=MESH)
    pl.semaphore_wait(barrier, 5 + groups - 1)

    gq = Gather(lambda lane, slot, rows: wq.at[lane, slot, rows], EVENTS, chunk, CUT_Q, qs, qr, near)
    go = Gather(
        lambda lane, slot, rows: wo.at[lane, slot, :, rows], EVENTS_O, half, CUT_O, os_, or_, {**near, "y": near["y3"]}
    )
    swap_o = pltpu.make_async_remote_copy(
        src_ref=wo_hbm.at[other_half],
        dst_ref=wo.at[0, 0, ylo],
        send_sem=ps.at[0],
        recv_sem=pr.at[0],
        device_id=near["yl"],
        device_id_type=MESH,
    )
    own_q.wait()
    gq.start(FIRST_A)
    gq.start(FIRST_B)

    def tok_copy(r):
        return pltpu.make_async_copy(tok_hbm.at[:, pl.ds(r * chunk, chunk)], tok.at[r], tsem.at[r])

    def kv_copy(r, slot):
        return pltpu.make_async_copy(wkv_hbm.at[pl.ds(r * chunk, chunk)], wkv.at[slot], ksem.at[slot])

    kv_copy(0, 0).start()
    for r in range(16):
        tok_copy(r).start()
    acc[...] = jnp.zeros_like(acc)

    @pl.loop(0, 16)
    def _(r):
        slot = r % 2

        @pl.when(r < 15)
        def _():
            kv_copy(r + 1, 1 - slot).start()

        tok_copy(r).wait()
        kv_copy(r, slot).wait()
        acc[:, 0:256] += jnp.dot(tok[r], wkv[slot], preferred_element_type=F32)

    kvs[...] = acc[:, 0:256].astype(BF16)
    acc[...] = jnp.zeros_like(acc)

    most = stretch.shape[1]
    lens = [new_ref[req, j] for j in range(groups)]
    ends = []
    for n in lens:
        ends.append(n if not ends else ends[-1] + n)
    ahead = lax.broadcasted_iota(jnp.int32, (most, count), 1) - lax.broadcasted_iota(jnp.int32, (most, count), 0)
    for d in range(0, groups, 8):
        picks = []
        for dest in range(d, d + 8):
            first = jnp.int32(0)
            for j in range(groups):
                first += jnp.where(route_ref[req, j] == dest, ends[j] - lens[j], 0)
            picks.append(jnp.where(ahead == first, 1.0, 0.0).astype(BF16))
        rows = jnp.dot(jnp.concatenate(picks, axis=0), kvs[...], preferred_element_type=F32)
        outgoing[d:d + 8] = rows.astype(BF16).reshape(8, most, 256)

    def handoff(i):
        to = (req + i) % groups
        return pltpu.make_async_remote_copy(
            src_ref=outgoing.at[to],
            dst_ref=stretch.at[req],
            send_sem=hs.at[i],
            recv_sem=hr.at[i],
            device_id=(tp, to),
            device_id_type=MESH,
        )

    for i in range(1, groups):
        handoff(i).start()
    stretch[req] = outgoing[req]

    def cache_copy(r):
        return pltpu.make_async_copy(cache_hbm.at[:, r], cbuf.at[r % 2], csem.at[r % 2])

    cache_copy(0).start()
    cache_copy(1).start()

    def decode(r):
        if r == 0:
            for i in range(1, groups):
                handoff(i).wait_recv()
        cache_copy(r).wait()
        slot = r % 2
        span = cbuf.shape[2]
        by_head = (((1,), (1,)), ((), ()))
        q = dq_ref[r]
        s = lax.dot_general(q, cbuf[slot, 0], by_head, preferred_element_type=F32) * scale
        col = lax.broadcasted_iota(jnp.int32, (32, span), 1)
        s = jnp.where(col < held_ref[0, r], s, NEG)
        keys = jnp.concatenate([stretch[r, :, 0:128], fresh_ref[r, 0]], axis=0)
        values = jnp.concatenate([stretch[r, :, 128:256], fresh_ref[r, 1]], axis=0)
        t = lax.dot_general(q, keys, by_head, preferred_element_type=F32) * scale
        col = lax.broadcasted_iota(jnp.int32, (32, 2 * most), 1)
        step = lax.broadcasted_iota(jnp.int32, (32, 2 * most), 0) >> 3
        given = jnp.int32(0)
        for j in range(groups):
            given += jnp.where(route_ref[r, j] == req, new_ref[r, j], 0)
        ok = (col < given) | ((col >= most) & (col - most <= step))
        t = jnp.where(ok, t, NEG)
        top = jnp.maximum(jnp.max(s, axis=1, keepdims=True), jnp.max(t, axis=1, keepdims=True))
        w = jnp.exp(s - top)
        f = jnp.exp(t - top)
        total = jnp.sum(w, axis=1, keepdims=True) + jnp.sum(f, axis=1, keepdims=True)
        got = jnp.dot(w.astype(BF16), cbuf[slot, 1], preferred_element_type=F32)
        got += jnp.dot(f.astype(BF16), values, preferred_element_type=F32)
        dec_ref[r] = (got / total).astype(BF16)
        if r + 2 < groups:
            cache_copy(r + 2).start()

    def place(slot):
        return (x + slot[0]) % 4, (yhi + slot[1]) % 2

    def query_unit(unit):
        slot = unit[0][1] * 4 + unit[0][0]
        xs, yhs = place(unit[0])
        start, size = row_range(unit[1], CUT_Q, chunk)
        gq.shared(*unit)

        @pl.loop(0, 8)
        def _(j):
            lane = j // 4
            cols = pl.ds(pl.multiple_of((j % 4) * 256, 256), 256)
            r = yhs * 8 + xs * 2 + c + lane * (1 - 2 * c)
            acc[:, cols] += jnp.dot(
                tok[r, :, start:start + size],
                wq[lane, slot, start:start + size, cols],
                preferred_element_type=F32,
            )

    query_unit(UNITS[0])
    query_unit(UNITS[1])
    waiting = []
    for k in range(len(EVENTS)):
        gq.event(k)
        if k == 1:
            swap_o.start()
        if k == START_O:
            own_o.wait()
            swap_o.wait_recv()
            go.start(START_1)
        if k == START_O + 1:
            go.start(START_2)
        for unit in waiting:
            query_unit(unit)
        waiting = EVENTS[k][2]
        if k >= 1:
            decode(k - 1)
    for unit in waiting:
        query_unit(unit)
    query[...] = acc[...].astype(BF16)

    def swap_mixed(b):
        rows = pl.ds(b * 256, 256)
        return pltpu.make_async_remote_copy(
            src_ref=mixed.at[ylo, rows],
            dst_ref=mixed.at[ylo, rows],
            send_sem=ms.at[b],
            recv_sem=mr.at[b],
            device_id=near["yl"],
            device_id_type=MESH,
        )

    for b in range(4):
        first = max(b - 1, 0) * 128
        rows = slice(b * 128, b * 128 + 128)
        q8 = jnp.concatenate([query[rows, h * 128:h * 128 + 128] for h in range(8)], axis=0)
        keys = kvs[first:first + 256, 0:128]
        values = kvs[first:first + 256, 128:256]
        s = lax.dot_general(q8, keys, (((1,), (1,)), ((), ())), preferred_element_type=F32) * scale
        row = lax.broadcasted_iota(jnp.int32, (128, 1), 0) + b * 128
        col = lax.broadcasted_iota(jnp.int32, (1, 256), 1) + first
        begin = jnp.zeros((128, 1), jnp.int32)
        for n, end in zip(lens, ends):
            begin += jnp.where(row >= end, n, 0)
        bias = jnp.where((col >= begin) & (col <= row), 0.0, NEG)
        s = (s.reshape(8, 128, 256) + bias[None]).reshape(1024, 256)
        w = jnp.exp(s - jnp.max(s, axis=1, keepdims=True))
        total = jnp.sum(w, axis=1, keepdims=True)
        o = jnp.dot(w.astype(BF16), values, preferred_element_type=F32) / total
        o = o.astype(BF16)
        for h in range(8):
            mixed[ylo, rows, h * 128:h * 128 + 128] = o[h * 128:h * 128 + 128]
        if b % 2 == 1:
            swap_mixed(b // 2).start()
        if b >= 1 and b < 3:
            go.event(b - 1)

    def role(slot):
        xs, yhs = place(slot)
        zs = yhs * 2 + xs // 2
        return (z + 4 - zs) % 4, zs, xs % 2

    def item(k):
        source, parts, row, rows = ITEMS[k]
        return source, source[1] * 4 + source[0], row, rows, *row_range(parts, CUT_O, half)

    def z_copy(k, dz):
        source, slot, row, rows, start, size = item(k)
        return pltpu.make_async_remote_copy(
            src_ref=tok.at[pl.ds(2 * slot, 2), pl.ds(row, rows), pl.ds(start, size)],
            dst_ref=rf.at[role(source)[2], dz - 1, :, pl.ds(row, rows), pl.ds(start, size)],
            send_sem=fs.at[k],
            recv_sem=fr.at[k, dz - 1],
            device_id=near["z%d" % (4 - dz)],
            device_id_type=MESH,
        )

    def out_cols(lane, start):
        return pl.multiple_of((c + lane * (1 - 2 * c)) * chunk + e * half + start, 128)

    def y_copy(k, lane):
        source, slot, row, rows, start, size = item(k)
        return pltpu.make_async_remote_copy(
            src_ref=tok.at[2 * slot + lane, pl.ds(row, rows), pl.ds(start, size)],
            dst_ref=out_ref.at[pl.ds(row, rows), pl.ds(out_cols(lane, start), size)],
            send_sem=ys.at[k, lane],
            recv_sem=yr.at[k, lane],
            device_id=near["yl"],
            device_id_type=MESH,
        )

    def part_item(k):
        source, slot, row, rows, start, size = item(k)
        if row == 0:
            go.shared(source, ITEMS[k][1])

        @pl.loop(0, 2)
        def _(lane):
            by_head = (((1,), (1,)), ((), ()))
            total = lax.dot_general(
                mixed[0, row:row + rows],
                wo[lane, slot, 0, start:start + size, :],
                by_head,
                preferred_element_type=F32,
            )
            total += lax.dot_general(
                mixed[1, row:row + rows],
                wo[lane, slot, 1, start:start + size, :],
                by_head,
                preferred_element_type=F32,
            )
            tok[2 * slot + lane, row:row + rows, start:start + size] = total.astype(BF16)

        dz, _, _ = role(source)
        for d in range(1, 4):

            @pl.when(dz == d)
            def _():
                z_copy(k, d).start()

    STEP = 64

    def collect(k):
        source, slot, row, rows, start, size = item(k)
        dz, _, ylos = role(source)

        @pl.when(dz == 0)
        def _():
            for d in range(1, 4):
                z_copy(k, d).wait_recv()

            def summed(j):
                lane = j // (rows // STEP)
                at = pl.ds(pl.multiple_of(row + (j % (rows // STEP)) * STEP, STEP), STEP)
                total = tok[2 * slot + lane, at, start:start + size].astype(F32)
                for d in range(3):
                    total += rf[ylos, d, lane, at, start:start + size].astype(F32)
                return lane, at, total.astype(BF16)

            @pl.when(ylos == ylo)
            def _():
                @pl.loop(0, 2 * (rows // STEP))
                def _(j):
                    lane, at, total = summed(j)
                    out_ref[at, pl.ds(out_cols(lane, start), size)] = total

            @pl.when(ylos != ylo)
            def _():
                @pl.loop(0, 2 * (rows // STEP))
                def _(j):
                    lane, at, total = summed(j)
                    tok[2 * slot + lane, at, start:start + size] = total

                for lane in range(2):
                    y_copy(k, lane).start()

    for what, k in PLAN:
        if what == "mixed":
            swap_mixed(k).wait_recv()
        elif what == "event":
            go.event(k)
        elif what == "part":
            part_item(k)
        elif what == "decode":
            decode(k)
        else:
            collect(k)

    gq.finish()
    go.finish()
    swap_o.wait_send()
    for i in range(1, groups):
        handoff(i).wait_send()
    for b in range(2):
        swap_mixed(b).wait_send()
    for k in range(len(ITEMS)):
        dz, _, ylos = role(ITEMS[k][0])
        for d in range(1, 4):

            @pl.when(dz == d)
            def _():
                z_copy(k, d).wait_send()

        @pl.when((dz == 0) & (ylos != ylo))
        def _():
            for lane in range(2):
                y_copy(k, lane).wait_send()

        @pl.when((dz == 0) & (ylos == ylo))
        def _():
            for lane in range(2):
                y_copy(k, lane).wait_recv()


def layer(tokens, wq, wkv, wo, cache, fresh, decode_query, cache_len, new_len, route):
    count, model = tokens.shape
    requests, most, span = (fresh.shape[0], fresh.shape[2], cache.shape[2])
    rows, cols = wq.shape
    any_ = pl.BlockSpec(memory_space=pl.ANY)
    vmem = pl.BlockSpec(memory_space=pltpu.VMEM)
    smem = pl.BlockSpec(memory_space=pltpu.SMEM)
    dma = pltpu.SemaphoreType.DMA
    n = len(ITEMS)
    return pl.pallas_call(
        layer_kernel,
        name="layer",
        out_shape=(
            jax.ShapeDtypeStruct((count, cols), BF16),
            jax.ShapeDtypeStruct(decode_query.shape, BF16),
        ),
        in_specs=[any_, any_, any_, any_, any_, vmem, vmem, smem, smem, smem],
        out_specs=(vmem, vmem),
        scratch_shapes=[
            pltpu.VMEM((16, count, 512), BF16),
            pltpu.VMEM((2, 8, rows, cols), BF16),
            pltpu.VMEM((2, 8, 2, rows // 2, cols), BF16),
            pltpu.VMEM((count, cols), F32),
            pltpu.VMEM((count, cols), BF16),
            pltpu.VMEM((2, count, cols), BF16),
            pltpu.VMEM((2, 3, 2, count, 256), BF16),
            pltpu.VMEM((2, 512, 256), BF16),
            pltpu.VMEM((count, 256), BF16),
            pltpu.VMEM((requests, most, 256), BF16),
            pltpu.VMEM((requests, most, 256), BF16),
            pltpu.VMEM((2, 2, span, 128), BF16),
            dma((len(MOVES_ALL),)), dma((len(MOVES_ALL),)), dma((len(MOVES_ALL),)), dma((len(MOVES_ALL),)),
            dma((2,)), dma((2,)), dma((1,)), dma((1,)),
            dma((n,)), dma((n, 3)), dma((n, 2)), dma((n, 2)),
            dma((16,)), dma((2,)), dma((2,)), dma((requests,)), dma((requests,)), dma((2,)),
        ],
        compiler_params=pltpu.CompilerParams(
            collective_id=0, has_side_effects=True, vmem_limit_bytes=63 * 2**20
        ),
    )(tokens, wq, wkv, wo, cache, fresh, decode_query, cache_len, new_len, route)


def local(
    tokens, w_query, w_keyval, output_weight, cache, fresh, decode_query, cache_len, new_len, route
):
    count, model = tokens.shape
    slots = route.shape[1]
    steps, rows, qcols = decode_query.shape
    width = w_keyval.shape[2] // 2
    heads = qcols // width
    most = 2 * count // slots
    extra = jnp.pad(jnp.transpose(fresh, (2, 0, 1, 3)), ((0, 0), (0, 0), (0, most - steps), (0, 0)))
    dq = decode_query.reshape(steps, rows, heads, width).transpose(1, 0, 2, 3).reshape(rows, steps * heads, width)
    prefill_out, decoded = layer(
        tokens,
        w_query.reshape(w_query.shape[0], -1),
        w_keyval.reshape(model, -1),
        output_weight.reshape(output_weight.shape[0], -1),
        cache,
        extra,
        dq,
        cache_len,
        new_len,
        route,
    )
    decode_out = decoded.reshape(rows, steps, heads, width).transpose(1, 0, 2, 3).reshape(steps, rows, qcols)
    return (prefill_out, decode_out)


def solution(mesh):
    placed = (
        P("req", None),
        P("req", "tp", None),
        P(None, "tp", None),
        P("req", "tp", None),
        P(None, "req", None, "tp"),
        P(None, None, "req", "tp"),
        P(None, "req", "tp"),
        P("req", None),
        P(),
        P(),
    )
    return jax.shard_map(
        local,
        mesh=mesh,
        in_specs=placed,
        out_specs=(P("req", "tp"), P(None, "req", "tp")),
        check_vma=False,
    )
```

time: 206 us -> 187 us (0.908)
  the two profiles are of different devices: /device:TPU:48 before, /device:TPU:78 now
where the time goes in v4:
time: 187 us
  Pallas kernels  179 us (96%)
  local copies, waits for them, and re-layouts  7.19 us (4%)
    pallas_call x1, Pallas kernels, layer(): pl.pallas_call(layer_kernel, name='layer', out_shape=(jax.ShapeDtypeStruc...  179 us
    unnamed x3, local copies, waits for them, and re-layouts  3.96 us

profile of v4, /device:TPU:78, one launch (start us, length us, event | category | flops | bytes accessed | tf_op | source)
XLA Modules:
  0.0 186.9 jit_solution(6035890973511748124)
XLA Ops:
  0.6 0.8 copy.19
  1.4 0.9 copy.16
  2.3 0.7 copy_bitcast_fusion.dq_ref
  3.0 0.9 pad.4.fresh_ref
  3.9 179.1 %layer.1 = (bf16[512,1024]{1,0:T(8,128)(2,1)}, bf16[16,32,128]{2,1,0:T(8,128)(2,1)}) custom-call(bf16[512,8192]{1,0:T(8,128)(2,1)} %tok_hbm.1, bf16[512,1024]{1,0:T(8,128)(2,1)} %bitcast.26, bf16[8192,256]{1,0:T(8,128)(2,1)} %bitcast.25, bf16[512,1024]{1,0:T(8,128)(2,1)} %bitcast.27, bf16[2,16,1024,128]{3,2,1,0:T(8,128)(2,1)} %cache_hbm.1, ...), custom_call_target="tpu_custom_call" | custom-call | tf_op jit(solution)/shard_map/layer/pallas_call | solution.py:516
  183.0 0.9 reshape.32
  184.0 0.7 copy.15
  184.7 2.3 %copy.21 = bf16[512,1024]{1,0:T(8,128)(2,1)} copy(bf16[512,1024]{1,0:T(8,128)(2,1)} %get-tuple-element.8) | data formatting | bytes 2097152

commit v5 on v4

--- a/solution.py
+++ b/solution.py
@@ -55,8 +55,8 @@
 EVENTS_O = [EVENTS[k] for k in (2, 0, 1, 5, 3, 4, 6, 7, 8, 9)]
 START_1 = ["xpB", "xmB", "yA", "s00B"]
 START_2 = ["xpA", "xmA", "yB0", "s00A"]
-EARLY = [((0, 0), "AB"), ((0, 1), "A"), ((3, 0), "AB"), ((1, 0), "AB")]
-LATE = [((3, 1), "A"), ((1, 1), "A"), ((2, 0), "AB"), ((0, 1), "B"), ((3, 1), "B"), ((1, 1), "B"), ((2, 1), "A"), ((2, 1), "B")]
+EARLY = [((0, 0), "AB"), ((0, 1), "AB"), ((3, 0), "AB"), ((1, 0), "AB")]
+LATE = [((3, 1), "AB"), ((1, 1), "AB"), ((2, 0), "AB"), ((2, 1), "A"), ((2, 1), "B")]
 ITEMS = [e + (r, 256) for r in (0, 256) for e in EARLY] + [e + (0, 512) for e in LATE]
 
 
@@ -65,10 +65,11 @@
 
 
 PLAN = (
-    [("event", 2), ("mixed", 0)] + span("part", 0, 2) + [("event", 3)] + span("part", 2, 4) + [("mixed", 1)] + span("part", 4, 8)
-    + [("event", 4)] + span("decode", 9, 13) + span("part", 8, 10) + [("event", 5), ("part", 10), ("event", 6), ("part", 11)]
-    + span("decode", 13, 16) + span("collect", 0, 4) + [("event", 7)] + span("part", 12, 14) + span("collect", 4, 8)
-    + [("event", 8), ("part", 14), ("event", 9), ("part", 15)] + span("collect", 8, 16)
+    [("event", 2), ("event", 6), ("mixed", 0)] + span("part", 0, 2) + [("event", 3)] + span("part", 2, 4) + [("mixed", 1)]
+    + span("pass", 0, 2) + span("part", 4, 8) + span("pass", 2, 4) + [("event", 4), ("event", 7)] + span("pass", 4, 6)
+    + span("part", 8, 10) + span("pass", 6, 8) + [("event", 5), ("part", 10)] + span("pass", 8, 10)
+    + span("collect", 0, 8) + [("event", 8), ("part", 11), ("pass", 10), ("event", 9), ("part", 12)]
+    + span("pass", 11, 13) + span("decode", 9, 16) + span("collect", 8, 13)
 )
 
 
@@ -150,8 +151,8 @@
 def layer_kernel(
     tok_hbm, wq_hbm, wkv_hbm, wo_hbm, cache_hbm, fresh_ref, dq_ref, held_ref, new_ref, route_ref,
     out_ref, dec_ref,
-    tok, wq, wo, acc, query, mixed, rf, wkv, kvs, outgoing, stretch, cbuf,
-    qs, qr, os_, or_, ms, mr, ps, pr, fs, fr, ys, yr, tsem, ksem, lsem, hs, hr, csem,
+    tok, wq, wo, acc, query, mixed, rh, rf, wkv, kvs, outgoing, stretch, cbuf,
+    qs, qr, os_, or_, ms, mr, ps, pr, hs2, hr2, fs, fr, ys, yr, tsem, ksem, lsem, hs, hr, csem,
 ):
     z, ylo, yhi, x, c = where_am_i()
     near = neighbours()
@@ -172,11 +173,11 @@
     req = yhi * 8 + x * 2 + c
     groups = stretch.shape[0]
     barrier = pltpu.get_barrier_semaphore()
-    for way in ("z1", "z2", "z3", "yl", "y3"):
+    for way in ("z1", "z3", "yl", "y3"):
         pl.semaphore_signal(barrier, inc=1, device_id=near[way], device_id_type=MESH)
     for i in range(1, groups):
         pl.semaphore_signal(barrier, inc=1, device_id=(tp, (req + i) % groups), device_id_type=MESH)
-    pl.semaphore_wait(barrier, 5 + groups - 1)
+    pl.semaphore_wait(barrier, 4 + groups - 1)
 
     gq = Gather(lambda lane, slot, rows: wq.at[lane, slot, rows], EVENTS, chunk, CUT_Q, qs, qr, near)
     go = Gather(
@@ -376,14 +377,26 @@
         source, parts, row, rows = ITEMS[k]
         return source, source[1] * 4 + source[0], row, rows, *row_range(parts, CUT_O, half)
 
-    def z_copy(k, dz):
+    def far_copy(k, which):
         source, slot, row, rows, start, size = item(k)
         return pltpu.make_async_remote_copy(
-            src_ref=tok.at[pl.ds(2 * slot, 2), pl.ds(row, rows), pl.ds(start, size)],
-            dst_ref=rf.at[role(source)[2], dz - 1, :, pl.ds(row, rows), pl.ds(start, size)],
-            send_sem=fs.at[k],
-            recv_sem=fr.at[k, dz - 1],
-            device_id=near["z%d" % (4 - dz)],
+            src_ref=tok.at[pl.ds(2 * slot, 2), pl.ds(row + which * (rows // 2), rows // 2), pl.ds(start, size)],
+            dst_ref=rh.at[slot, :, pl.ds(row // 2, rows // 2), pl.ds(start, size)],
+            send_sem=hs2.at[k, which],
+            recv_sem=hr2.at[k, which],
+            device_id=near["z3" if which else "z1"],
+            device_id_type=MESH,
+        )
+
+    def near_copy(k, which, part):
+        source, slot, row, rows, start, size = item(k)
+        at = pl.ds(row + part * (rows // 2), rows // 2)
+        return pltpu.make_async_remote_copy(
+            src_ref=tok.at[pl.ds(2 * slot, 2), at, pl.ds(start, size)],
+            dst_ref=rf.at[role(source)[2], which, :, at, pl.ds(start, size)],
+            send_sem=fs.at[k, part],
+            recv_sem=fr.at[k, which * 2 + part],
+            device_id=near["z3" if which else "z1"],
             device_id_type=MESH,
         )
 
@@ -424,13 +437,40 @@
             tok[2 * slot + lane, row:row + rows, start:start + size] = total.astype(BF16)
 
         dz, _, _ = role(source)
-        for d in range(1, 4):
-
-            @pl.when(dz == d)
+
+        @pl.when(dz == 2)
+        def _():
+            far_copy(k, 0).start()
+            far_copy(k, 1).start()
+
+        for which in range(2):
+
+            @pl.when(dz == (1 if which else 3))
             def _():
-                z_copy(k, d).start()
+                near_copy(k, which, 1 - which).start()
 
     STEP = 64
+
+    def pass_on(k):
+        source, slot, row, rows, start, size = item(k)
+        dz, _, _ = role(source)
+        for which in range(2):
+
+            @pl.when(dz == (1 if which else 3))
+            def _():
+                far_copy(k, which).wait_recv()
+                steps = rows // 2 // STEP
+
+                @pl.loop(0, 2 * steps)
+                def _(j):
+                    lane = j // steps
+                    i = pl.multiple_of((j % steps) * STEP, STEP)
+                    at = pl.ds(row + which * (rows // 2) + i, STEP)
+                    total = tok[2 * slot + lane, at, start:start + size].astype(F32)
+                    total += rh[slot, lane, pl.ds(row // 2 + i, STEP), start:start + size].astype(F32)
+                    tok[2 * slot + lane, at, start:start + size] = total.astype(BF16)
+
+                near_copy(k, which, which).start()
 
     def collect(k):
         source, slot, row, rows, start, size = item(k)
@@ -438,14 +478,15 @@
 
         @pl.when(dz == 0)
         def _():
-            for d in range(1, 4):
-                z_copy(k, d).wait_recv()
+            for which in range(2):
+                for part in range(2):
+                    near_copy(k, which, part).wait_recv()
 
             def summed(j):
                 lane = j // (rows // STEP)
                 at = pl.ds(pl.multiple_of(row + (j % (rows // STEP)) * STEP, STEP), STEP)
                 total = tok[2 * slot + lane, at, start:start + size].astype(F32)
-                for d in range(3):
+                for d in range(2):
                     total += rf[ylos, d, lane, at, start:start + size].astype(F32)
                 return lane, at, total.astype(BF16)
 
@@ -473,6 +514,8 @@
             go.event(k)
         elif what == "part":
             part_item(k)
+        elif what == "pass":
+            pass_on(k)
         elif what == "decode":
             decode(k)
         else:
@@ -487,11 +530,18 @@
         swap_mixed(b).wait_send()
     for k in range(len(ITEMS)):
         dz, _, ylos = role(ITEMS[k][0])
-        for d in range(1, 4):
-
-            @pl.when(dz == d)
+
+        @pl.when(dz == 2)
+        def _():
+            far_copy(k, 0).wait_send()
+            far_copy(k, 1).wait_send()
+
+        for which in range(2):
+
+            @pl.when(dz == (1 if which else 3))
             def _():
-                z_copy(k, d).wait_send()
+                near_copy(k, which, 0).wait_send()
+                near_copy(k, which, 1).wait_send()
 
         @pl.when((dz == 0) & (ylos != ylo))
         def _():
@@ -529,7 +579,8 @@
             pltpu.VMEM((count, cols), F32),
             pltpu.VMEM((count, cols), BF16),
             pltpu.VMEM((2, count, cols), BF16),
-            pltpu.VMEM((2, 3, 2, count, 256), BF16),
+            pltpu.VMEM((8, 2, count // 2, 256), BF16),
+            pltpu.VMEM((2, 2, 2, count, 256), BF16),
             pltpu.VMEM((2, 512, 256), BF16),
             pltpu.VMEM((count, 256), BF16),
             pltpu.VMEM((requests, most, 256), BF16),
@@ -537,7 +588,7 @@
             pltpu.VMEM((2, 2, span, 128), BF16),
             dma((len(MOVES_ALL),)), dma((len(MOVES_ALL),)), dma((len(MOVES_ALL),)), dma((len(MOVES_ALL),)),
             dma((2,)), dma((2,)), dma((1,)), dma((1,)),
-            dma((n,)), dma((n, 3)), dma((n, 2)), dma((n, 2)),
+            dma((n, 2)), dma((n, 2)), dma((n, 2)), dma((n, 4)), dma((n, 2)), dma((n, 2)),
             dma((16,)), dma((2,)), dma((2,)), dma((requests,)), dma((requests,)), dma((2,)),
         ],
         compiler_params=pltpu.CompilerParams(

time: 187 us -> 174 us (0.930)
  the two profiles are of different devices: /device:TPU:78 before, /device:TPU:24 now
where the time goes in v5:
time: 174 us
  Pallas kernels  166 us (95%)
  local copies, waits for them, and re-layouts  7.19 us (4%)
    pallas_call x1, Pallas kernels, layer(): pl.pallas_call(layer_kernel, name='layer', out_shape=(jax.ShapeDtypeStruc...  166 us
    unnamed x3, local copies, waits for them, and re-layouts  3.96 us

profile of v5, /device:TPU:24, one launch (start us, length us, event | category | flops | bytes accessed | tf_op | source)
XLA Modules:
  0.0 174.0 jit_solution(14193495650692022825)
XLA Ops:
  0.6 0.8 copy.19
  1.4 0.9 copy.16
  2.3 0.7 copy_bitcast_fusion.dq_ref
  3.0 0.9 pad.4.fresh_ref
  3.9 166.1 %layer.1 = (bf16[512,1024]{1,0:T(8,128)(2,1)}, bf16[16,32,128]{2,1,0:T(8,128)(2,1)}) custom-call(bf16[512,8192]{1,0:T(8,128)(2,1)} %tok_hbm.1, bf16[512,1024]{1,0:T(8,128)(2,1)} %bitcast.26, bf16[8192,256]{1,0:T(8,128)(2,1)} %bitcast.25, bf16[512,1024]{1,0:T(8,128)(2,1)} %bitcast.27, bf16[2,16,1024,128]{3,2,1,0:T(8,128)(2,1)} %cache_hbm.1, ...), custom_call_target="tpu_custom_call" | custom-call | tf_op jit(solution)/shard_map/layer/pallas_call | solution.py:566
  170.0 0.9 reshape.32
  171.0 0.7 copy.15
  171.7 2.3 %copy.21 = bf16[512,1024]{1,0:T(8,128)(2,1)} copy(bf16[512,1024]{1,0:T(8,128)(2,1)} %get-tuple-element.8) | data formatting | bytes 2097152

commit v6 on v5

--- a/solution.py
+++ b/solution.py
@@ -151,7 +151,7 @@
 def layer_kernel(
     tok_hbm, wq_hbm, wkv_hbm, wo_hbm, cache_hbm, fresh_ref, dq_ref, held_ref, new_ref, route_ref,
     out_ref, dec_ref,
-    tok, wq, wo, acc, query, mixed, rh, rf, wkv, kvs, outgoing, stretch, cbuf,
+    tok, wq, wo, acc, query, mixed, rh, rf, wkv, kvs, outgoing, stretch, cbuf, dec,
     qs, qr, os_, or_, ms, mr, ps, pr, hs2, hr2, fs, fr, ys, yr, tsem, ksem, lsem, hs, hr, csem,
 ):
     z, ylo, yhi, x, c = where_am_i()
@@ -286,7 +286,10 @@
         total = jnp.sum(w, axis=1, keepdims=True) + jnp.sum(f, axis=1, keepdims=True)
         got = jnp.dot(w.astype(BF16), cbuf[slot, 1], preferred_element_type=F32)
         got += jnp.dot(f.astype(BF16), values, preferred_element_type=F32)
-        dec_ref[r] = (got / total).astype(BF16)
+        got = got / total
+        for t_ in range(dec.shape[0]):
+            for h in range(8):
+                dec[t_, r:r + 1, h * 128:h * 128 + 128] = got[t_ * 8 + h:t_ * 8 + h + 1]
         if r + 2 < groups:
             cache_copy(r + 2).start()
 
@@ -521,6 +524,7 @@
         else:
             collect(k)
 
+    dec_ref[...] = dec[...].astype(BF16)
     gq.finish()
     go.finish()
     swap_o.wait_send()
@@ -562,13 +566,14 @@
     vmem = pl.BlockSpec(memory_space=pltpu.VMEM)
     smem = pl.BlockSpec(memory_space=pltpu.SMEM)
     dma = pltpu.SemaphoreType.DMA
+    out_dec = (decode_query.shape[1] // 8, requests, 8 * 128)
     n = len(ITEMS)
     return pl.pallas_call(
         layer_kernel,
         name="layer",
         out_shape=(
             jax.ShapeDtypeStruct((count, cols), BF16),
-            jax.ShapeDtypeStruct(decode_query.shape, BF16),
+            jax.ShapeDtypeStruct(out_dec, BF16),
         ),
         in_specs=[any_, any_, any_, any_, any_, vmem, vmem, smem, smem, smem],
         out_specs=(vmem, vmem),
@@ -586,6 +591,7 @@
             pltpu.VMEM((requests, most, 256), BF16),
             pltpu.VMEM((requests, most, 256), BF16),
             pltpu.VMEM((2, 2, span, 128), BF16),
+            pltpu.VMEM(out_dec, F32),
             dma((len(MOVES_ALL),)), dma((len(MOVES_ALL),)), dma((len(MOVES_ALL),)), dma((len(MOVES_ALL),)),
             dma((2,)), dma((2,)), dma((1,)), dma((1,)),
             dma((n, 2)), dma((n, 2)), dma((n, 2)), dma((n, 4)), dma((n, 2)), dma((n, 2)),
@@ -620,8 +626,7 @@
         new_len,
         route,
     )
-    decode_out = decoded.reshape(rows, steps, heads, width).transpose(1, 0, 2, 3).reshape(steps, rows, qcols)
-    return (prefill_out, decode_out)
+    return (prefill_out, decoded)
 
 
 def solution(mesh):

time: 174 us -> 174 us (level)
    unnamed x3 -> x4, local copies, waits for them, and re-layouts: 3.96 us -> 5.53 us
where the time goes in v6:
time: 174 us
  Pallas kernels  166 us (95%)
  local copies, waits for them, and re-layouts  7.12 us (4%)
    pallas_call x1, Pallas kernels, layer(): pl.pallas_call(layer_kernel, name='layer', out_shape=(jax.ShapeDtypeStruc...  166 us
    unnamed x4, local copies, waits for them, and re-layouts  5.53 us

profile of v6, /device:TPU:24, one launch (start us, length us, event | category | flops | bytes accessed | tf_op | source)
XLA Modules:
  0.0 173.9 jit_solution(6888316269018860832)
XLA Ops:
  0.6 0.8 copy.17
  1.4 0.9 copy.14
  2.3 0.7 copy_bitcast_fusion.dq_ref
  3.0 0.9 pad.4.fresh_ref
  3.9 166.1 %layer.1 = (bf16[512,1024]{1,0:T(8,128)(2,1)}, bf16[4,16,1024]{2,1,0:T(8,128)(2,1)}) custom-call(bf16[512,8192]{1,0:T(8,128)(2,1)} %tok_hbm.1, bf16[512,1024]{1,0:T(8,128)(2,1)} %bitcast.19, bf16[8192,256]{1,0:T(8,128)(2,1)} %bitcast.18, bf16[512,1024]{1,0:T(8,128)(2,1)} %bitcast.20, bf16[2,16,1024,128]{3,2,1,0:T(8,128)(2,1)} %cache_hbm.1, ...), custom_call_target="tpu_custom_call" | custom-call | tf_op jit(solution)/shard_map/layer/pallas_call | solution.py:571
  170.1 2.3 %copy.20 = bf16[512,1024]{1,0:T(8,128)(2,1)} copy(bf16[512,1024]{1,0:T(8,128)(2,1)} %get-tuple-element.4) | data formatting | bytes 2097152
  172.3 1.6 copy.21
